TPU v7x, 512 devices: a whole 4x8x8 slice. The times are simulated.
512 devices in a mesh: energy: 128 (over y_hi, z, x), slab: 4 (over y_lo, core).
Axes of the slice: x: 4, y: 8 (y_hi: 4, y_lo: 2; y = y_hi * 2 + y_lo), z: 8, core: 2. Of those that a mesh axis runs over, the one named last changes fastest.
Arguments:
- green_blocks: bfloat16 [128, 4, 512, 512], P('energy', 'slab'), may hold values from -6 to 6
- coulomb: bfloat16 [4, 512, 512], P('slab'), may hold values from -0.25 to 0.25
- couple_cols: int32 [4, 128, 8], P('slab'), may hold values from 0 to 127
- couple_vals: bfloat16 [4, 128, 8], P('slab'), may hold values from -0.8984375 to 0.8984375
Outputs:
- new_green: bfloat16 [128, 4, 512, 512], P('energy', 'slab')
Inputs may be any that keep to these rules, and one draw needn't show every extreme that they name: couple_cols[s, i, k] names one of the first 128 orbitals of slab s + 1.
All inputs are finite; a program needn't handle non-finite values.
Results may differ from a plain program's by a relative error of at most 0.015.
Values may be sent and summed in bfloat16 or wider, within the bound.
No kernel may reach another device: no remote copies, remote signals or barrier semaphores. Data moves between devices by JAX's collectives and lax.ppermute only.
A program may use at most 64 MiB of HBM per device.

v0:
```python
import functools
import math

import jax
import jax.numpy as jnp
import ml_dtypes
import numpy as np
from jax import lax
from jax.experimental import pallas as pl
from jax.experimental.pallas import tpu as pltpu
from jax.sharding import PartitionSpec as P

BLOCK = 128
ROWS = 8
OWNERS = BLOCK // ROWS
LIMIT = 40 * 1024 * 1024


def pairs_of(blocks):
    apart = [(a, b) for a in range(blocks) for b in range(a + 1, blocks)]
    return apart, [(a, a + 1) for a in range(0, blocks, 2)]


def dot(left, right):
    return jnp.dot(left, right, preferred_element_type=jnp.float32)


def parts(values):
    high = values.astype(jnp.bfloat16)
    return high, (values - high.astype(jnp.float32)).astype(jnp.bfloat16)


def triangle():
    row = lax.broadcasted_iota(jnp.int32, (BLOCK, BLOCK), 0)
    column = lax.broadcasted_iota(jnp.int32, (BLOCK, BLOCK), 1)
    return row <= column, row < column


def pack(block, blocks, out_ref):
    apart, diagonal = pairs_of(blocks)
    upper, above = triangle()
    for p, (a, b) in enumerate(apart + diagonal):
        if p < len(apart):
            first, second = block(a, b), block(b, a).T
        else:
            one, two = block(a, a), block(b, b)
            first, second = jnp.where(upper, one, two), jnp.where(above, one.T, two.T)
        both = jnp.concatenate(
            [first.reshape(OWNERS, ROWS, BLOCK), second.reshape(OWNERS, ROWS, BLOCK)], axis=1
        )
        out_ref[p * OWNERS : (p + 1) * OWNERS] = both.astype(jnp.bfloat16)


def unpack(in_ref, blocks, store):
    apart, diagonal = pairs_of(blocks)
    upper, _ = triangle()
    for p, (a, b) in enumerate(apart + diagonal):
        both = in_ref[p * OWNERS : (p + 1) * OWNERS].astype(jnp.float32)
        first = both[:, :ROWS].reshape(BLOCK, BLOCK)
        second = both[:, ROWS:].reshape(BLOCK, BLOCK).T
        if p < len(apart):
            store(a, b, first)
            store(b, a, second)
        else:
            store(a, a, jnp.where(upper, first, second))
            store(b, b, jnp.where(upper, second, first))


def at(a, b):
    return pl.ds(a * BLOCK, BLOCK), pl.ds(b * BLOCK, BLOCK)


def pack_kernel(blocks, green_ref, out_ref):
    pack(lambda a, b: green_ref[at(a, b)].astype(jnp.float32), blocks, out_ref)


def forward(table_ref, entries):
    return dot(table_ref[...], jnp.concatenate([entries, entries], axis=0))


def backward(table_ref, real, imag):
    high, low = parts(jnp.concatenate([real, imag], axis=0))
    return dot(table_ref[...], jnp.concatenate([high, low, high], axis=0))


def polar_kernel(entries_ref, own_ref, forward_ref, backward_ref, spectrum_ref, out_ref):
    spectrum = forward(forward_ref, entries_ref[...])
    spectrum_ref[...] = spectrum
    half, width = spectrum.shape[0] // 2, spectrum.shape[1] // 2
    edge = lax.broadcasted_iota(jnp.int32, (half, width), 0) == 0
    own = own_ref[...] > 0.5
    real = spectrum[:half, :width], spectrum[:half, width:]
    imag = spectrum[half:, :width], spectrum[half:, width:]
    for slot in range(2):
        mirror_real = jnp.where(own, real[slot], real[1 - slot])
        mirror_imag = jnp.where(own, imag[slot], imag[1 - slot])
        rr, ii = real[slot] * mirror_real, imag[slot] * mirror_imag
        ir, ri = imag[slot] * mirror_real, real[slot] * mirror_imag
        values = backward(backward_ref, jnp.where(edge, rr, rr + ii), jnp.where(edge, ii, ir - ri))
        out_ref[:, slot * width : (slot + 1) * width] = values.astype(jnp.bfloat16)


def screen_kernel(blocks, polar_ref, coulomb_ref, out_ref, matrix_ref, screened_ref):
    def store(a, b, value):
        matrix_ref[at(a, b)] = value.astype(jnp.bfloat16)

    unpack(polar_ref, blocks, store)
    coulomb = coulomb_ref[...]
    inner = dot(coulomb, matrix_ref[...]).astype(jnp.bfloat16)
    second = dot(inner, coulomb)
    third = dot(inner, second.astype(jnp.bfloat16))
    screened = (coulomb.astype(jnp.float32) + second + third).astype(jnp.bfloat16)
    screened_ref[...] = screened.astype(jnp.float32)
    pack(lambda a, b: screened_ref[at(a, b)], blocks, out_ref)


def sigma_kernel(entries_ref, green_ref, forward_ref, backward_ref, out_ref):
    spectrum = forward(forward_ref, entries_ref[...])
    half = spectrum.shape[0] // 2
    edge = lax.broadcasted_iota(jnp.int32, (half, spectrum.shape[1]), 0) == 0
    real, imag = spectrum[:half], spectrum[half:]
    green_real, green_imag = green_ref[:half], green_ref[half:]
    rr, ii = green_real * real, green_imag * imag
    cross = green_real * imag + green_imag * real
    values = backward(backward_ref, jnp.where(edge, rr, rr - ii), jnp.where(edge, ii, cross))
    out_ref[...] = values.astype(jnp.bfloat16)


def final_kernel(blocks, inv_root, sigma_ref, green_ref, right_ref, left_ref, out_ref, total_ref):
    def store(a, b, value):
        if a == b == blocks - 1:
            value = value + right_ref[...]
        if a == b == 0:
            value = value + left_ref[...]
        total_ref[at(a, b)] = value.astype(jnp.bfloat16)

    unpack(sigma_ref, blocks, store)
    green = green_ref[...]
    dressed = dot(green, total_ref[...]).astype(jnp.bfloat16)
    updated = green.astype(jnp.float32) + dot(dressed, green) * inv_root
    out_ref[...] = updated.astype(jnp.bfloat16)


def call(kernel, outs, scratch=(), flops=0, moved=0):
    return pl.pallas_call(
        kernel,
        out_shape=outs,
        scratch_shapes=list(scratch),
        compiler_params=pltpu.CompilerParams(vmem_limit_bytes=LIMIT),
        cost_estimate=pl.CostEstimate(flops=flops, bytes_accessed=moved, transcendentals=0),
    )


def tables(energies, scale):
    half = energies // 2
    turns = np.outer(np.arange(half), np.arange(energies)) % energies
    angle = turns * (2.0 * math.pi / energies)
    cosine, sine = np.cos(angle), -np.sin(angle)
    sine[0] = np.cos(math.pi * np.arange(energies))
    weights = np.full((half, 1), 2.0 / energies)
    weights[0] = 1.0 / energies
    ahead = np.concatenate([cosine, sine], axis=0)
    back = np.concatenate([cosine * weights, sine * weights], axis=0).T

    def two(table):
        high = table.astype(ml_dtypes.bfloat16)
        return high, (table - high.astype(np.float64)).astype(ml_dtypes.bfloat16)

    ahead_high, ahead_low = two(ahead)
    result = [np.concatenate([ahead_high, ahead_low], axis=1)]
    for factor in scale:
        high, low = two(back * factor)
        result.append(np.concatenate([high, high, low], axis=1))
    return [jnp.asarray(t) for t in result]


def coupling_matrix(column_ids, coupling_values):
    width = column_ids.shape[0]
    hits = column_ids[:, :, None] == jnp.arange(width, dtype=jnp.int32)[None, None, :]
    summed = jnp.sum(
        jnp.where(hits, coupling_values.astype(jnp.float32)[:, :, None], jnp.float32(0.0)), axis=1
    )
    return summed.astype(jnp.bfloat16)


def from_behind(x, axis, by):
    size = lax.axis_size(axis)
    pairs = [(i, i + by) for i in range(size) if 0 <= i + by < size]
    return lax.ppermute(x, axis, pairs)


def exchange(x):
    return lax.all_to_all(x, "energy", split_axis=0, concat_axis=0, tiled=True)


def on_device(green_blocks, coulomb, couple_cols, couple_vals):
    green, coulomb_block = green_blocks[0, 0], coulomb[0]
    orbitals = green.shape[0]
    blocks = orbitals // BLOCK
    energies = lax.axis_size("energy")
    chunk = (energies, 2 * ROWS, BLOCK)
    flat = (energies, 2 * ROWS * BLOCK)
    f32, b16 = jnp.float32, jnp.bfloat16
    ahead, back_polar, back_sigma = tables(
        energies, (0.5 / math.sqrt(orbitals * energies), 0.2 / math.sqrt(energies))
    )

    packed = call(functools.partial(pack_kernel, blocks), jax.ShapeDtypeStruct(chunk, b16))(green)
    entries = exchange(packed).reshape(flat)

    owner = lax.axis_index("energy")
    column = jnp.arange(ROWS * BLOCK, dtype=jnp.int32)
    row = lax.rem(owner, OWNERS) * ROWS + column // BLOCK
    shares = owner >= energies - (blocks // 2) * OWNERS
    own = ((row == column % BLOCK) & shares).astype(f32)[None]

    spectrum, polar = call(
        polar_kernel, (jax.ShapeDtypeStruct(flat, f32), jax.ShapeDtypeStruct(flat, b16))
    )(entries, own, ahead, back_polar)
    polar = exchange(polar.reshape(chunk))

    screened = call(
        functools.partial(screen_kernel, blocks),
        jax.ShapeDtypeStruct(chunk, b16),
        (pltpu.VMEM((orbitals, orbitals), b16), pltpu.VMEM((orbitals, orbitals), f32)),
    )(polar, coulomb_block)
    screened = exchange(screened).reshape(flat)

    sigma = call(sigma_kernel, jax.ShapeDtypeStruct(flat, b16))(
        screened, spectrum, ahead, back_sigma
    )
    sigma = exchange(sigma.reshape(chunk))

    interface = couple_cols.shape[1]
    last = orbitals - interface
    inv_root = 1.0 / math.sqrt(orbitals)
    coupling = coupling_matrix(couple_cols[0], couple_vals[0])
    behind = from_behind(jnp.concatenate([green[last:, last:], coupling], axis=0), "slab", 1)
    prev_corner, previous = behind[:interface], behind[interface:]
    next_corner = from_behind(green[:interface, :interface], "slab", -1)
    near_next = dot(coupling, next_corner).astype(b16)
    near_prev = dot(previous.T, prev_corner).astype(b16)
    right_part = dot(near_next, coupling.T) * inv_root
    left_part = dot(near_prev, previous) * inv_root

    updated = call(
        functools.partial(final_kernel, blocks, inv_root),
        jax.ShapeDtypeStruct((orbitals, orbitals), b16),
        (pltpu.VMEM((orbitals, orbitals), b16),),
    )(sigma, green, right_part, left_part)
    return updated[None, None]


def solution(mesh):
    return jax.shard_map(
        on_device,
        mesh=mesh,
        in_specs=(
            P("energy", "slab", None, None),
            P("slab", None, None),
            P("slab", None, None),
            P("slab", None, None),
        ),
        out_specs=P("energy", "slab", None, None),
        check_vma=False,
    )
```

profile of v0, /device:TPU:1, one launch (start us, length us, event | category | flops | bytes accessed | tf_op | source)
XLA Modules:
  0.0 135.6 jit_solution(3216878446703369499)
XLA Ops:
  0.0 1.0 copy-done
  1.0 1.0 shard_map.73
  2.0 20.8 %all-to-all-start = ((bf16[128,16,128]{2,1,0:T(8,128)(2,1)}), bf16[128,16,128]{2,1,0:T(8,128)(2,1)S(1)}, u32[]{:S(2)}, u32[]{:S(2)}) async-start(bf16[128,16,128]{2,1,0:T(8,128)(2,1)} %shard_map.73), calls=%async_computation | async-start | bytes 1048576 | tf_op jit(solution)/shard_map/all_to_all | solution.py:193
  22.9 20.8 %all-to-all-done = bf16[128,16,128]{2,1,0:T(8,128)(2,1)S(1)} async-done(((bf16[128,16,128]{2,1,0:T(8,128)(2,1)}), bf16[128,16,128]{2,1,0:T(8,128)(2,1)S(1)}, u32[]{:S(2)}, u32[]{:S(2)}) %all-to-all-start) | async-done | bytes 524320 | tf_op jit(solution)/shard_map/all_to_all | solution.py:193
  43.7 0.1 copy.19
  43.8 0.7 copy-done.3
  44.6 1.0 shard_map.74
  45.7 28.3 %all_to_all.20.polar_ref = bf16[128,16,128]{2,1,0:T(8,128)(2,1)S(1)} all-to-all(bf16[128,16,128]{2,1,0:T(8,128)(2,1)S(1)} %bitcast.31), channel_id=1, replica_groups=mesh['energy'=128,'slab'=4] {'energy'}, dimensions={0} | all-to-all | bytes 1048576 | tf_op jit(solution)/shard_map/all_to_all | solution.py:193
  74.0 1.3 shard_map.75
  75.3 28.0 %all_to_all.21 = bf16[128,16,128]{2,1,0:T(8,128)(2,1)S(1)} all-to-all(bf16[128,16,128]{2,1,0:T(8,128)(2,1)S(1)} %shard_map.75), channel_id=1, replica_groups=mesh['energy'=128,'slab'=4] {'energy'}, dimensions={0} | all-to-all | bytes 1048576 | tf_op jit(solution)/shard_map/all_to_all | solution.py:193
  103.3 0.1 copy.18
  103.4 0.7 copy-done.4
  104.2 0.8 shard_map.76
  105.0 0.9 copy.15
  105.9 7.2 %all-to-all-start.3 = ((bf16[128,16,128]{2,1,0:T(8,128)(2,1)}), bf16[128,16,128]{2,1,0:T(8,128)(2,1)S(1)}, u32[]{:S(2)}, u32[]{:S(2)}) async-start(bf16[128,16,128]{2,1,0:T(8,128)(2,1)} %bitcast.13), calls=%async_computation.3 | async-start | bytes 1048576 | tf_op jit(solution)/shard_map/all_to_all | solution.py:193
  113.2 3.4 %collective-permute-start = (bf16[128,128]{1,0:T(8,128)(2,1)S(1)}, bf16[128,128]{1,0:T(8,128)(2,1)S(1)}, u32[]{:S(2)}, u32[]{:S(2)}) collective-permute-start(bf16[128,128]{1,0:T(8,128)(2,1)S(1)} %get-tuple-element.10), channel_id=1, source_target_pairs={{1,0},{2,1},{3,2},{5,4},{6,5},{7,6},{9,8},{10,9},{11,10},{13,12},{... | collective-permute-start | bytes 98312 | tf_op jit(solution)/shard_map/ppermute | solution.py:189
  116.9 0.4 select_reduce_fusion
  117.2 2.1 %collective-permute-start.1 = (bf16[256,128]{1,0:T(8,128)(2,1)S(1)}, bf16[256,128]{1,0:T(8,128)(2,1)S(1)}, u32[]{:S(2)}, u32[]{:S(2)}) collective-permute-start(bf16[256,128]{1,0:T(8,128)(2,1)S(1)} %pad_maximum_fusion), channel_id=1, source_target_pairs={{0,1},{1,2},{2,3},{4,5},{5,6},{6,7},{8,9},{9,10},{10,11},{12,13},{... | collective-permute-start | bytes 196616 | tf_op jit(solution)/shard_map/ppermute | solution.py:189
  119.4 2.7 %collective-permute-done = bf16[128,128]{1,0:T(8,128)(2,1)S(1)} collective-permute-done((bf16[128,128]{1,0:T(8,128)(2,1)S(1)}, bf16[128,128]{1,0:T(8,128)(2,1)S(1)}, u32[]{:S(2)}, u32[]{:S(2)}) %collective-permute-start) | collective-permute-done | bytes 32800 | tf_op jit(solution)/shard_map/ppermute | solution.py:189
  122.1 0.3 convolution_multiply_fusion.1.right_ref
  122.3 1.9 %collective-permute-done.1 = bf16[256,128]{1,0:T(8,128)(2,1)S(1)} collective-permute-done((bf16[256,128]{1,0:T(8,128)(2,1)S(1)}, bf16[256,128]{1,0:T(8,128)(2,1)S(1)}, u32[]{:S(2)}, u32[]{:S(2)}) %collective-permute-start.1) | collective-permute-done | bytes 65568 | tf_op jit(solution)/shard_map/ppermute | solution.py:189
  124.2 0.3 convolution_multiply_fusion.left_ref
  124.5 9.4 %all-to-all-done.3.sigma_ref = bf16[128,16,128]{2,1,0:T(8,128)(2,1)S(1)} async-done(((bf16[128,16,128]{2,1,0:T(8,128)(2,1)}), bf16[128,16,128]{2,1,0:T(8,128)(2,1)S(1)}, u32[]{:S(2)}, u32[]{:S(2)}) %all-to-all-start.3) | async-done | bytes 524320 | tf_op jit(solution)/shard_map/all_to_all | solution.py:193
  134.0 1.6 %shard_map.77 = bf16[512,512]{1,0:T(8,128)(2,1)} custom-call(bf16[128,16,128]{2,1,0:T(8,128)(2,1)S(1)} %all-to-all-done.3.sigma_ref, bf16[512,512]{1,0:T(8,128)(2,1)S(1)} %bitcast.24, f32[128,128]{1,0:T(8,128)S(1)} %convolution_multiply_fusion.1.right_ref, f32[128,128]{1,0:T(8,128)S(1)} %convolution_multiply_fusion.left_ref), custom_call_target="tpu_custom_call" | custom-call | tf_op jit(solution)/shard_map/pallas_call | solution.py:246
  (20 shorter events, 0.5 us)
Async XLA Ops:
  0.0 1.0 copy-start
  2.0 41.7 %all-to-all-start = ((bf16[128,16,128]{2,1,0:T(8,128)(2,1)}), bf16[128,16,128]{2,1,0:T(8,128)(2,1)S(1)}, u32[]{:S(2)}, u32[]{:S(2)}) async-start(bf16[128,16,128]{2,1,0:T(8,128)(2,1)} %shard_map.73), calls=%async_computation | async-start | bytes 1048576 | tf_op jit(solution)/shard_map/all_to_all | solution.py:193
  43.7 0.8 copy-start.3
  43.7 0.9 copy-start.5
  45.7 28.3 %copy-start.2 = (bf16[1,512,512]{2,1,0:T(8,128)(2,1)S(1)}, bf16[1,512,512]{2,1,0:T(8,128)(2,1)}, u32[]{:S(2)}) copy-start(bf16[1,512,512]{2,1,0:T(8,128)(2,1)} %param.8) | copy-start | bytes 1572868
  103.3 0.9 copy-start.4
  105.9 7.2 %copy-start.1 = (bf16[1,1,512,512]{3,2,1,0:T(8,128)(2,1)S(1)}, bf16[1,1,512,512]{3,2,1,0:T(8,128)(2,1)}, u32[]{:S(2)}) copy-start(bf16[1,1,512,512]{3,2,1,0:T(8,128)(2,1)} %param.7) | copy-start | bytes 1572868
  105.9 10.7 %copy-start.7 = (bf16[1,128,8]{1,2,0:T(8,128)(2,1)S(1)}, bf16[1,128,8]{1,2,0:T(8,128)(2,1)}, u32[]{:S(2)}) copy-start(bf16[1,128,8]{1,2,0:T(8,128)(2,1)} %param.10) | copy-start | bytes 6148
  105.9 28.0 %all-to-all-start.3 = ((bf16[128,16,128]{2,1,0:T(8,128)(2,1)}), bf16[128,16,128]{2,1,0:T(8,128)(2,1)S(1)}, u32[]{:S(2)}, u32[]{:S(2)}) async-start(bf16[128,16,128]{2,1,0:T(8,128)(2,1)} %bitcast.13), calls=%async_computation.3 | async-start | bytes 1048576 | tf_op jit(solution)/shard_map/all_to_all | solution.py:193
  113.2 3.6 %copy-start.6 = (s32[1,128,8]{1,2,0:T(8,128)S(1)}, s32[1,128,8]{1,2,0:T(8,128)}, u32[]{:S(2)}) copy-start(s32[1,128,8]{1,2,0:T(8,128)} %param.9) | copy-start | bytes 12292
  113.2 8.9 %collective-permute-start = (bf16[128,128]{1,0:T(8,128)(2,1)S(1)}, bf16[128,128]{1,0:T(8,128)(2,1)S(1)}, u32[]{:S(2)}, u32[]{:S(2)}) collective-permute-start(bf16[128,128]{1,0:T(8,128)(2,1)S(1)} %get-tuple-element.10), channel_id=1, source_target_pairs={{1,0},{2,1},{3,2},{5,4},{6,5},{7,6},{9,8},{10,9},{11,10},{13,12},{... | collective-permute-start | bytes 98312 | tf_op jit(solution)/shard_map/ppermute | solution.py:189
  117.2 7.0 %collective-permute-start.1 = (bf16[256,128]{1,0:T(8,128)(2,1)S(1)}, bf16[256,128]{1,0:T(8,128)(2,1)S(1)}, u32[]{:S(2)}, u32[]{:S(2)}) collective-permute-start(bf16[256,128]{1,0:T(8,128)(2,1)S(1)} %pad_maximum_fusion), channel_id=1, source_target_pairs={{0,1},{1,2},{2,3},{4,5},{5,6},{6,7},{8,9},{9,10},{10,11},{12,13},{... | collective-permute-start | bytes 196616 | tf_op jit(solution)/shard_map/ppermute | solution.py:189
where the time goes:
time: 136 us
  blocking collectives  56.3 us (41%)
  waiting for transfers between devices  34.8 us (26%)
  starting transfers between devices  33.6 us (25%)
  Pallas kernels  5.66 us (4%)
  local copies, waits for them, and re-layouts  4.1 us (3%)
    all_to_all x2, blocking collectives, exchange(): return lax.all_to_all(x, 'energy', split_axis=0, concat_axis=0, tiled=True)  56.3 us
    all_to_all x2, waiting for transfers between devices, exchange(): return lax.all_to_all(x, 'energy', split_axis=0, concat_axis=0, tiled=True)  30.2 us
    all_to_all x2, starting transfers between devices, exchange(): return lax.all_to_all(x, 'energy', split_axis=0, concat_axis=0, tiled=True)  28.1 us
    ppermute x2, starting transfers between devices, from_behind(): return lax.ppermute(x, axis, pairs)  5.56 us
    ppermute x2, waiting for transfers between devices, from_behind(): return lax.ppermute(x, axis, pairs)  4.58 us
    unnamed x20, local copies, waits for them, and re-layouts  3.89 us
  transfers between devices with their start and end apart: 4, of which 4 were waited for; matrix products, arithmetic and copies ran while one was open for 1% of the time, Pallas kernels for 0%

commit v1 on v0

--- a/solution.py
+++ b/solution.py
@@ -3,8 +3,6 @@
 
 import jax
 import jax.numpy as jnp
-import ml_dtypes
-import numpy as np
 from jax import lax
 from jax.experimental import pallas as pl
 from jax.experimental.pallas import tpu as pltpu
@@ -83,7 +81,7 @@
     return dot(table_ref[...], jnp.concatenate([high, low, high], axis=0))
 
 
-def polar_kernel(entries_ref, own_ref, forward_ref, backward_ref, spectrum_ref, out_ref):
+def polar_kernel(scale, entries_ref, own_ref, forward_ref, backward_ref, spectrum_ref, out_ref):
     spectrum = forward(forward_ref, entries_ref[...])
     spectrum_ref[...] = spectrum
     half, width = spectrum.shape[0] // 2, spectrum.shape[1] // 2
@@ -97,7 +95,7 @@
         rr, ii = real[slot] * mirror_real, imag[slot] * mirror_imag
         ir, ri = imag[slot] * mirror_real, real[slot] * mirror_imag
         values = backward(backward_ref, jnp.where(edge, rr, rr + ii), jnp.where(edge, ii, ir - ri))
-        out_ref[:, slot * width : (slot + 1) * width] = values.astype(jnp.bfloat16)
+        out_ref[:, slot * width : (slot + 1) * width] = (values * scale).astype(jnp.bfloat16)
 
 
 def screen_kernel(blocks, polar_ref, coulomb_ref, out_ref, matrix_ref, screened_ref):
@@ -114,7 +112,7 @@
     pack(lambda a, b: screened_ref[at(a, b)], blocks, out_ref)
 
 
-def sigma_kernel(entries_ref, green_ref, forward_ref, backward_ref, out_ref):
+def sigma_kernel(scale, entries_ref, green_ref, forward_ref, backward_ref, out_ref):
     spectrum = forward(forward_ref, entries_ref[...])
     half = spectrum.shape[0] // 2
     edge = lax.broadcasted_iota(jnp.int32, (half, spectrum.shape[1]), 0) == 0
@@ -123,7 +121,7 @@
     rr, ii = green_real * real, green_imag * imag
     cross = green_real * imag + green_imag * real
     values = backward(backward_ref, jnp.where(edge, rr, rr - ii), jnp.where(edge, ii, cross))
-    out_ref[...] = values.astype(jnp.bfloat16)
+    out_ref[...] = (values * scale).astype(jnp.bfloat16)
 
 
 def final_kernel(blocks, inv_root, sigma_ref, green_ref, right_ref, left_ref, out_ref, total_ref):
@@ -151,27 +149,22 @@
     )
 
 
-def tables(energies, scale):
+def tables(energies):
     half = energies // 2
-    turns = np.outer(np.arange(half), np.arange(energies)) % energies
-    angle = turns * (2.0 * math.pi / energies)
-    cosine, sine = np.cos(angle), -np.sin(angle)
-    sine[0] = np.cos(math.pi * np.arange(energies))
-    weights = np.full((half, 1), 2.0 / energies)
-    weights[0] = 1.0 / energies
-    ahead = np.concatenate([cosine, sine], axis=0)
-    back = np.concatenate([cosine * weights, sine * weights], axis=0).T
-
-    def two(table):
-        high = table.astype(ml_dtypes.bfloat16)
-        return high, (table - high.astype(np.float64)).astype(ml_dtypes.bfloat16)
-
-    ahead_high, ahead_low = two(ahead)
-    result = [np.concatenate([ahead_high, ahead_low], axis=1)]
-    for factor in scale:
-        high, low = two(back * factor)
-        result.append(np.concatenate([high, high, low], axis=1))
-    return [jnp.asarray(t) for t in result]
+    frequency = jnp.arange(half, dtype=jnp.int32)
+    energy = jnp.arange(energies, dtype=jnp.int32)
+    turns = (frequency[:, None] * energy[None, :]) % energies
+    angle = turns.astype(jnp.float32) * (2.0 * math.pi / energies)
+    first = frequency[:, None] == 0
+    cosine = jnp.cos(angle)
+    sine = jnp.where(first, (1 - 2 * (energy % 2)).astype(jnp.float32)[None], -jnp.sin(angle))
+    weights = jnp.where(first, 1.0, 2.0).astype(jnp.float32) / energies
+    ahead_high, ahead_low = parts(jnp.concatenate([cosine, sine], axis=0))
+    back_high, back_low = parts(jnp.concatenate([cosine * weights, sine * weights], axis=0).T)
+    return (
+        jnp.concatenate([ahead_high, ahead_low], axis=1),
+        jnp.concatenate([back_high, back_high, back_low], axis=1),
+    )
 
 
 def coupling_matrix(column_ids, coupling_values):
@@ -201,22 +194,36 @@
     chunk = (energies, 2 * ROWS, BLOCK)
     flat = (energies, 2 * ROWS * BLOCK)
     f32, b16 = jnp.float32, jnp.bfloat16
-    ahead, back_polar, back_sigma = tables(
-        energies, (0.5 / math.sqrt(orbitals * energies), 0.2 / math.sqrt(energies))
-    )
-
     packed = call(functools.partial(pack_kernel, blocks), jax.ShapeDtypeStruct(chunk, b16))(green)
-    entries = exchange(packed).reshape(flat)
-
+    packed, corners = lax.optimization_barrier((packed, green))
+    entries = exchange(packed)
+
+    ahead, back = tables(energies)
     owner = lax.axis_index("energy")
     column = jnp.arange(ROWS * BLOCK, dtype=jnp.int32)
     row = lax.rem(owner, OWNERS) * ROWS + column // BLOCK
     shares = owner >= energies - (blocks // 2) * OWNERS
     own = ((row == column % BLOCK) & shares).astype(f32)[None]
 
+    interface = couple_cols.shape[1]
+    last = orbitals - interface
+    inv_root = 1.0 / math.sqrt(orbitals)
+    coupling = coupling_matrix(couple_cols[0], couple_vals[0])
+    behind = from_behind(jnp.concatenate([corners[last:, last:], coupling], axis=0), "slab", 1)
+    prev_corner, previous = behind[:interface], behind[interface:]
+    next_corner = from_behind(corners[:interface, :interface], "slab", -1)
+    near_next = dot(coupling, next_corner).astype(b16)
+    near_prev = dot(previous.T, prev_corner).astype(b16)
+    right_part = dot(near_next, coupling.T) * inv_root
+    left_part = dot(near_prev, previous) * inv_root
+    entries, ahead, back, own, right_part, left_part = lax.optimization_barrier(
+        (entries, ahead, back, own, right_part, left_part)
+    )
+
     spectrum, polar = call(
-        polar_kernel, (jax.ShapeDtypeStruct(flat, f32), jax.ShapeDtypeStruct(flat, b16))
-    )(entries, own, ahead, back_polar)
+        functools.partial(polar_kernel, 0.5 / math.sqrt(orbitals * energies)),
+        (jax.ShapeDtypeStruct(flat, f32), jax.ShapeDtypeStruct(flat, b16)),
+    )(entries.reshape(flat), own, ahead, back)
     polar = exchange(polar.reshape(chunk))
 
     screened = call(
@@ -226,22 +233,11 @@
     )(polar, coulomb_block)
     screened = exchange(screened).reshape(flat)
 
-    sigma = call(sigma_kernel, jax.ShapeDtypeStruct(flat, b16))(
-        screened, spectrum, ahead, back_sigma
-    )
+    sigma = call(
+        functools.partial(sigma_kernel, 0.2 / math.sqrt(energies)),
+        jax.ShapeDtypeStruct(flat, b16),
+    )(screened, spectrum, ahead, back)
     sigma = exchange(sigma.reshape(chunk))
-
-    interface = couple_cols.shape[1]
-    last = orbitals - interface
-    inv_root = 1.0 / math.sqrt(orbitals)
-    coupling = coupling_matrix(couple_cols[0], couple_vals[0])
-    behind = from_behind(jnp.concatenate([green[last:, last:], coupling], axis=0), "slab", 1)
-    prev_corner, previous = behind[:interface], behind[interface:]
-    next_corner = from_behind(green[:interface, :interface], "slab", -1)
-    near_next = dot(coupling, next_corner).astype(b16)
-    near_prev = dot(previous.T, prev_corner).astype(b16)
-    right_part = dot(near_next, coupling.T) * inv_root
-    left_part = dot(near_prev, previous) * inv_root
 
     updated = call(
         functools.partial(final_kernel, blocks, inv_root),

time: 136 us -> 133 us (0.978)
  blocking collectives: 56.3 us -> 84 us
  waiting for transfers between devices: 34.8 us -> 12.4 us
  starting transfers between devices: 33.6 us -> 26.5 us
  local copies, waits for them, and re-layouts: 4.1 us -> 2.45 us
    all_to_all x2 -> x3, blocking collectives: 56.3 us -> 84 us  [exchange(): return lax.all_to_all(x, 'energy', split_axis=0, concat_axis=0, tiled=True)]
    all_to_all x2 -> x1, waiting for transfers between devices: 30.2 us -> 8.33 us  [exchange(): return lax.all_to_all(x, 'energy', split_axis=0, concat_axis=0, tiled=True)]
    all_to_all x2 -> x1, starting transfers between devices: 28.1 us -> 20.9 us  [exchange(): return lax.all_to_all(x, 'energy', split_axis=0, concat_axis=0, tiled=True)]
    unnamed x20 -> x14, local copies, waits for them, and re-layouts: 3.89 us -> 2.14 us
  transfers between devices with their start and end apart: 4 -> 3, of which waited for: 4 -> 2; matrix products, arithmetic and copies ran while one was open for 1% -> 2% of each run, Pallas kernels for 0% -> 0%
where the time goes in v1:
time: 133 us
  blocking collectives  84 us (63%)
  starting transfers between devices  26.5 us (20%)
  waiting for transfers between devices  12.4 us (9%)
  Pallas kernels  5.65 us (4%)
  local copies, waits for them, and re-layouts  2.45 us (2%)
    all_to_all x3, blocking collectives, exchange(): return lax.all_to_all(x, 'energy', split_axis=0, concat_axis=0, tiled=True)  84 us
    all_to_all x1, starting transfers between devices, exchange(): return lax.all_to_all(x, 'energy', split_axis=0, concat_axis=0, tiled=True)  20.9 us
    all_to_all x1, waiting for transfers between devices, exchange(): return lax.all_to_all(x, 'energy', split_axis=0, concat_axis=0, tiled=True)  8.33 us
    ppermute x2, starting transfers between devices, from_behind(): return lax.ppermute(x, axis, pairs)  5.56 us
    ppermute x2, waiting for transfers between devices, from_behind(): return lax.ppermute(x, axis, pairs)  4.05 us
  transfers between devices with their start and end apart: 3, of which 2 were waited for; matrix products, arithmetic and copies ran while one was open for 2% of the time, Pallas kernels for 0%

profile of v1, /device:TPU:1, one launch (start us, length us, event | category | flops | bytes accessed | tf_op | source)
XLA Modules:
  0.0 133.1 jit_solution(3084138926201867271)
XLA Ops:
  0.0 1.0 copy-done
  1.0 1.0 shard_map.46
  2.0 20.9 %all-to-all-start = ((bf16[128,16,128]{2,1,0:T(8,128)(2,1)}), bf16[128,16,128]{2,1,0:T(8,128)(2,1)S(1)}, u32[]{:S(2)}, u32[]{:S(2)}) async-start(bf16[128,16,128]{2,1,0:T(8,128)(2,1)} %shard_map.46), calls=%async_computation | async-start | bytes 1048576 | tf_op jit(solution)/shard_map/all_to_all | solution.py:186
  23.0 2.9 %collective-permute-start = (bf16[128,128]{1,0:T(8,128)(2,1)S(1)}, bf16[128,128]{1,0:T(8,128)(2,1)S(1)}, u32[]{:S(2)}, u32[]{:S(2)}) collective-permute-start(bf16[128,128]{1,0:T(8,128)(2,1)S(1)} %get-tuple-element.26), channel_id=1, source_target_pairs={{1,0},{2,1},{3,2},{5,4},{6,5},{7,6},{9,8},{10,9},{11,10},{13,12},{... | collective-permute-start | bytes 98312 | tf_op jit(solution)/shard_map/ppermute | solution.py:182
  26.0 0.6 copy-done.3
  26.7 0.4 select_reduce_fusion
  27.1 2.7 %collective-permute-start.1 = (bf16[256,128]{1,0:T(8,128)(2,1)S(1)}, bf16[256,128]{1,0:T(8,128)(2,1)S(1)}, u32[]{:S(2)}, u32[]{:S(2)}) collective-permute-start(bf16[256,128]{1,0:T(8,128)(2,1)S(1)} %pad_maximum_fusion.3), channel_id=1, source_target_pairs={{0,1},{1,2},{2,3},{4,5},{5,6},{6,7},{8,9},{9,10},{10,11},{12,13},{... | collective-permute-start | bytes 196616 | tf_op jit(solution)/shard_map/ppermute | solution.py:182
  29.8 0.3 fusion.10
  30.1 0.3 broadcast_multiply_fusion
  30.7 4.1 %collective-permute-done = bf16[128,128]{1,0:T(8,128)(2,1)S(1)} collective-permute-done((bf16[128,128]{1,0:T(8,128)(2,1)S(1)}, bf16[128,128]{1,0:T(8,128)(2,1)S(1)}, u32[]{:S(2)}, u32[]{:S(2)}) %collective-permute-start) | collective-permute-done | bytes 32800 | tf_op jit(solution)/shard_map/ppermute | solution.py:182
  34.8 0.3 convolution_multiply_fusion.1.right_ref
  35.0 0.3 convolution_multiply_fusion.left_ref
  35.3 8.3 %all-to-all-done = bf16[128,16,128]{2,1,0:T(8,128)(2,1)S(1)} async-done(((bf16[128,16,128]{2,1,0:T(8,128)(2,1)}), bf16[128,16,128]{2,1,0:T(8,128)(2,1)S(1)}, u32[]{:S(2)}, u32[]{:S(2)}) %all-to-all-start) | async-done | bytes 524320 | tf_op jit(solution)/shard_map/all_to_all | solution.py:186
  43.7 0.1 copy.20
  43.9 0.9 shard_map.47
  44.9 0.1 copy.14
  45.0 28.4 %all_to_all.20.polar_ref = bf16[128,16,128]{2,1,0:T(8,128)(2,1)S(1)} all-to-all(bf16[128,16,128]{2,1,0:T(8,128)(2,1)S(1)} %bitcast.39), channel_id=1, replica_groups=mesh['energy'=128,'slab'=4] {'energy'}, dimensions={0} | all-to-all | bytes 1048576 | tf_op jit(solution)/shard_map/all_to_all | solution.py:186
  73.5 1.3 shard_map.48
  74.8 28.0 %all_to_all.21 = bf16[128,16,128]{2,1,0:T(8,128)(2,1)S(1)} all-to-all(bf16[128,16,128]{2,1,0:T(8,128)(2,1)S(1)} %shard_map.48), channel_id=1, replica_groups=mesh['energy'=128,'slab'=4] {'energy'}, dimensions={0} | all-to-all | bytes 1048576 | tf_op jit(solution)/shard_map/all_to_all | solution.py:186
  102.7 0.1 copy.19
  102.9 0.8 shard_map.49
  103.7 0.1 copy.16
  103.8 27.6 %all_to_all.22.sigma_ref = bf16[128,16,128]{2,1,0:T(8,128)(2,1)S(1)} all-to-all(bf16[128,16,128]{2,1,0:T(8,128)(2,1)S(1)} %bitcast.41), channel_id=1, replica_groups=mesh['energy'=128,'slab'=4] {'energy'}, dimensions={0} | all-to-all | bytes 1048576 | tf_op jit(solution)/shard_map/all_to_all | solution.py:186
  131.4 1.6 %shard_map.50 = bf16[512,512]{1,0:T(8,128)(2,1)} custom-call(bf16[128,16,128]{2,1,0:T(8,128)(2,1)S(1)} %all_to_all.22.sigma_ref, bf16[512,512]{1,0:T(8,128)(2,1)S(1)} %bitcast.32, f32[128,128]{1,0:T(8,128)S(1)} %convolution_multiply_fusion.1.right_ref, f32[128,128]{1,0:T(8,128)S(1)} %convolution_multiply_fusion.left_ref), custom_call_target="tpu_custom_call" | custom-call | tf_op jit(solution)/shard_map/pallas_call | solution.py:242
  (24 shorter events, 0.7 us)
Async XLA Ops:
  0.0 1.0 copy-start
  2.0 21.0 %copy-start.1 = (bf16[1,1,512,512]{3,2,1,0:T(8,128)(2,1)S(1)}, bf16[1,1,512,512]{3,2,1,0:T(8,128)(2,1)}, u32[]{:S(2)}) copy-start(bf16[1,1,512,512]{3,2,1,0:T(8,128)(2,1)} %param.4) | copy-start | bytes 1572868
  2.0 41.7 %all-to-all-start = ((bf16[128,16,128]{2,1,0:T(8,128)(2,1)}), bf16[128,16,128]{2,1,0:T(8,128)(2,1)S(1)}, u32[]{:S(2)}, u32[]{:S(2)}) async-start(bf16[128,16,128]{2,1,0:T(8,128)(2,1)} %shard_map.46), calls=%async_computation | async-start | bytes 1048576 | tf_op jit(solution)/shard_map/all_to_all | solution.py:186
  23.0 2.9 %copy-start.4 = (bf16[1,128,8]{1,2,0:T(8,128)(2,1)S(1)}, bf16[1,128,8]{1,2,0:T(8,128)(2,1)}, u32[]{:S(2)}) copy-start(bf16[1,128,8]{1,2,0:T(8,128)(2,1)} %param.7) | copy-start | bytes 6148
  23.0 11.8 %collective-permute-start = (bf16[128,128]{1,0:T(8,128)(2,1)S(1)}, bf16[128,128]{1,0:T(8,128)(2,1)S(1)}, u32[]{:S(2)}, u32[]{:S(2)}) collective-permute-start(bf16[128,128]{1,0:T(8,128)(2,1)S(1)} %get-tuple-element.26), channel_id=1, source_target_pairs={{1,0},{2,1},{3,2},{5,4},{6,5},{7,6},{9,8},{10,9},{11,10},{13,12},{... | collective-permute-start | bytes 98312 | tf_op jit(solution)/shard_map/ppermute | solution.py:182
  25.9 0.7 copy-start.3
  27.1 8.0 %collective-permute-start.1 = (bf16[256,128]{1,0:T(8,128)(2,1)S(1)}, bf16[256,128]{1,0:T(8,128)(2,1)S(1)}, u32[]{:S(2)}, u32[]{:S(2)}) collective-permute-start(bf16[256,128]{1,0:T(8,128)(2,1)S(1)} %pad_maximum_fusion.3), channel_id=1, source_target_pairs={{0,1},{1,2},{2,3},{4,5},{5,6},{6,7},{8,9},{9,10},{10,11},{12,13},{... | collective-permute-start | bytes 196616 | tf_op jit(solution)/shard_map/ppermute | solution.py:182
  45.0 28.5 %copy-start.2 = (bf16[1,512,512]{2,1,0:T(8,128)(2,1)S(1)}, bf16[1,512,512]{2,1,0:T(8,128)(2,1)}, u32[]{:S(2)}) copy-start(bf16[1,512,512]{2,1,0:T(8,128)(2,1)} %param.5) | copy-start | bytes 1572868

commit v2 on v1

--- a/solution.py
+++ b/solution.py
@@ -73,12 +73,12 @@
 
 
 def forward(table_ref, entries):
-    return dot(table_ref[...], jnp.concatenate([entries, entries], axis=0))
+    return dot(table_ref[...], entries)
 
 
 def backward(table_ref, real, imag):
     high, low = parts(jnp.concatenate([real, imag], axis=0))
-    return dot(table_ref[...], jnp.concatenate([high, low, high], axis=0))
+    return dot(table_ref[...], jnp.concatenate([high, low], axis=0))
 
 
 def polar_kernel(scale, entries_ref, own_ref, forward_ref, backward_ref, spectrum_ref, out_ref):
@@ -151,20 +151,21 @@
 
 def tables(energies):
     half = energies // 2
-    frequency = jnp.arange(half, dtype=jnp.int32)
-    energy = jnp.arange(energies, dtype=jnp.int32)
-    turns = (frequency[:, None] * energy[None, :]) % energies
-    angle = turns.astype(jnp.float32) * (2.0 * math.pi / energies)
-    first = frequency[:, None] == 0
-    cosine = jnp.cos(angle)
-    sine = jnp.where(first, (1 - 2 * (energy % 2)).astype(jnp.float32)[None], -jnp.sin(angle))
-    weights = jnp.where(first, 1.0, 2.0).astype(jnp.float32) / energies
-    ahead_high, ahead_low = parts(jnp.concatenate([cosine, sine], axis=0))
-    back_high, back_low = parts(jnp.concatenate([cosine * weights, sine * weights], axis=0).T)
-    return (
-        jnp.concatenate([ahead_high, ahead_low], axis=1),
-        jnp.concatenate([back_high, back_high, back_low], axis=1),
-    )
+
+    def waves(shape, along):
+        row = lax.broadcasted_iota(jnp.int32, shape, along)
+        energy = lax.broadcasted_iota(jnp.int32, shape, 1 - along)
+        frequency = row % half
+        angle = ((frequency * energy) % energies).astype(jnp.float32) * (2.0 * math.pi / energies)
+        nyquist = (1 - 2 * (energy % 2)).astype(jnp.float32)
+        sine = jnp.where(frequency == 0, nyquist, -jnp.sin(angle))
+        return jnp.where(row < half, jnp.cos(angle), sine), frequency == 0
+
+    square = (energies, energies)
+    ahead, _ = waves(square, 0)
+    back, first = waves(square, 1)
+    back = (back * (jnp.where(first, 1.0, 2.0) / energies)).astype(jnp.bfloat16)
+    return ahead.astype(jnp.bfloat16), jnp.concatenate([back, back], axis=1)
 
 
 def coupling_matrix(column_ids, coupling_values):

time: 133 us -> 133 us (level)
  transfers between devices with their start and end apart: 3 -> 3, of which waited for: 2 -> 2; matrix products, arithmetic and copies ran while one was open for 2% -> 1% of each run, Pallas kernels for 0% -> 0%
where the time goes in v2:
time: 133 us
  blocking collectives  84 us (63%)
  starting transfers between devices  26.5 us (20%)
  waiting for transfers between devices  12.6 us (9%)
  Pallas kernels  5.36 us (4%)
  local copies, waits for them, and re-layouts  2.35 us (2%)
    all_to_all x3, blocking collectives, exchange(): return lax.all_to_all(x, 'energy', split_axis=0, concat_axis=0, tiled=True)  84 us
    all_to_all x1, starting transfers between devices, exchange(): return lax.all_to_all(x, 'energy', split_axis=0, concat_axis=0, tiled=True)  20.9 us
    all_to_all x1, waiting for transfers between devices, exchange(): return lax.all_to_all(x, 'energy', split_axis=0, concat_axis=0, tiled=True)  8.33 us
    ppermute x2, starting transfers between devices, from_behind(): return lax.ppermute(x, axis, pairs)  5.56 us
    ppermute x2, waiting for transfers between devices, from_behind(): return lax.ppermute(x, axis, pairs)  4.3 us
  transfers between devices with their start and end apart: 3, of which 2 were waited for; matrix products, arithmetic and copies ran while one was open for 1% of the time, Pallas kernels for 0%

profile of v2, /device:TPU:1, one launch (start us, length us, event | category | flops | bytes accessed | tf_op | source)
XLA Modules:
  0.0 132.6 jit_solution(4631227939984567628)
XLA Ops:
  0.0 1.0 copy-done
  1.0 1.0 shard_map.46
  2.0 20.9 %all-to-all-start = ((bf16[128,16,128]{2,1,0:T(8,128)(2,1)}), bf16[128,16,128]{2,1,0:T(8,128)(2,1)S(1)}, u32[]{:S(2)}, u32[]{:S(2)}) async-start(bf16[128,16,128]{2,1,0:T(8,128)(2,1)} %shard_map.46), calls=%async_computation | async-start | bytes 1048576 | tf_op jit(solution)/shard_map/all_to_all | solution.py:187
  23.0 2.9 %collective-permute-start = (bf16[128,128]{1,0:T(8,128)(2,1)S(1)}, bf16[128,128]{1,0:T(8,128)(2,1)S(1)}, u32[]{:S(2)}, u32[]{:S(2)}) collective-permute-start(bf16[128,128]{1,0:T(8,128)(2,1)S(1)} %get-tuple-element.26), channel_id=1, source_target_pairs={{1,0},{2,1},{3,2},{5,4},{6,5},{7,6},{9,8},{10,9},{11,10},{13,12},{... | collective-permute-start | bytes 98312 | tf_op jit(solution)/shard_map/ppermute | solution.py:183
  25.9 0.1 copy.8
  26.0 0.6 copy-done.3
  26.7 0.4 select_reduce_fusion
  27.1 2.7 %collective-permute-start.1 = (bf16[256,128]{1,0:T(8,128)(2,1)S(1)}, bf16[256,128]{1,0:T(8,128)(2,1)S(1)}, u32[]{:S(2)}, u32[]{:S(2)}) collective-permute-start(bf16[256,128]{1,0:T(8,128)(2,1)S(1)} %pad_maximum_fusion.1), channel_id=1, source_target_pairs={{0,1},{1,2},{2,3},{4,5},{5,6},{6,7},{8,9},{9,10},{10,11},{12,13},{... | collective-permute-start | bytes 196616 | tf_op jit(solution)/shard_map/ppermute | solution.py:183
  29.8 0.6 fusion.4
  30.5 4.3 %collective-permute-done = bf16[128,128]{1,0:T(8,128)(2,1)S(1)} collective-permute-done((bf16[128,128]{1,0:T(8,128)(2,1)S(1)}, bf16[128,128]{1,0:T(8,128)(2,1)S(1)}, u32[]{:S(2)}, u32[]{:S(2)}) %collective-permute-start) | collective-permute-done | bytes 32800 | tf_op jit(solution)/shard_map/ppermute | solution.py:183
  34.8 0.3 convolution_multiply_fusion.1.right_ref
  35.0 0.3 convolution_multiply_fusion.left_ref
  35.3 8.3 %all-to-all-done = bf16[128,16,128]{2,1,0:T(8,128)(2,1)S(1)} async-done(((bf16[128,16,128]{2,1,0:T(8,128)(2,1)}), bf16[128,16,128]{2,1,0:T(8,128)(2,1)S(1)}, u32[]{:S(2)}, u32[]{:S(2)}) %all-to-all-start) | async-done | bytes 524320 | tf_op jit(solution)/shard_map/all_to_all | solution.py:187
  43.7 0.1 copy.16
  43.8 0.8 shard_map.47
  44.6 0.1 copy.10
  44.7 28.4 %all_to_all.20.polar_ref = bf16[128,16,128]{2,1,0:T(8,128)(2,1)S(1)} all-to-all(bf16[128,16,128]{2,1,0:T(8,128)(2,1)S(1)} %bitcast.31), channel_id=1, replica_groups=mesh['energy'=128,'slab'=4] {'energy'}, dimensions={0} | all-to-all | bytes 1048576 | tf_op jit(solution)/shard_map/all_to_all | solution.py:187
  73.2 1.3 shard_map.48
  74.5 28.0 %all_to_all.21 = bf16[128,16,128]{2,1,0:T(8,128)(2,1)S(1)} all-to-all(bf16[128,16,128]{2,1,0:T(8,128)(2,1)S(1)} %shard_map.48), channel_id=1, replica_groups=mesh['energy'=128,'slab'=4] {'energy'}, dimensions={0} | all-to-all | bytes 1048576 | tf_op jit(solution)/shard_map/all_to_all | solution.py:187
  102.4 0.1 copy.15
  102.6 0.7 shard_map.49
  103.3 0.1 copy.12
  103.4 27.6 %all_to_all.22.sigma_ref = bf16[128,16,128]{2,1,0:T(8,128)(2,1)S(1)} all-to-all(bf16[128,16,128]{2,1,0:T(8,128)(2,1)S(1)} %bitcast.33), channel_id=1, replica_groups=mesh['energy'=128,'slab'=4] {'energy'}, dimensions={0} | all-to-all | bytes 1048576 | tf_op jit(solution)/shard_map/all_to_all | solution.py:187
  131.0 1.6 %shard_map.50 = bf16[512,512]{1,0:T(8,128)(2,1)} custom-call(bf16[128,16,128]{2,1,0:T(8,128)(2,1)S(1)} %all_to_all.22.sigma_ref, bf16[512,512]{1,0:T(8,128)(2,1)S(1)} %bitcast.24, f32[128,128]{1,0:T(8,128)S(1)} %convolution_multiply_fusion.1.right_ref, f32[128,128]{1,0:T(8,128)S(1)} %convolution_multiply_fusion.left_ref), custom_call_target="tpu_custom_call" | custom-call | tf_op jit(solution)/shard_map/pallas_call | solution.py:243
  (19 shorter events, 0.2 us)
Async XLA Ops:
  0.0 1.0 copy-start
  2.0 21.0 %copy-start.1 = (bf16[1,1,512,512]{3,2,1,0:T(8,128)(2,1)S(1)}, bf16[1,1,512,512]{3,2,1,0:T(8,128)(2,1)}, u32[]{:S(2)}) copy-start(bf16[1,1,512,512]{3,2,1,0:T(8,128)(2,1)} %param.4) | copy-start | bytes 1572868
  2.0 41.7 %all-to-all-start = ((bf16[128,16,128]{2,1,0:T(8,128)(2,1)}), bf16[128,16,128]{2,1,0:T(8,128)(2,1)S(1)}, u32[]{:S(2)}, u32[]{:S(2)}) async-start(bf16[128,16,128]{2,1,0:T(8,128)(2,1)} %shard_map.46), calls=%async_computation | async-start | bytes 1048576 | tf_op jit(solution)/shard_map/all_to_all | solution.py:187
  23.0 2.9 %copy-start.4 = (bf16[1,128,8]{1,2,0:T(8,128)(2,1)S(1)}, bf16[1,128,8]{1,2,0:T(8,128)(2,1)}, u32[]{:S(2)}) copy-start(bf16[1,128,8]{1,2,0:T(8,128)(2,1)} %param.7) | copy-start | bytes 6148
  23.0 11.8 %collective-permute-start = (bf16[128,128]{1,0:T(8,128)(2,1)S(1)}, bf16[128,128]{1,0:T(8,128)(2,1)S(1)}, u32[]{:S(2)}, u32[]{:S(2)}) collective-permute-start(bf16[128,128]{1,0:T(8,128)(2,1)S(1)} %get-tuple-element.26), channel_id=1, source_target_pairs={{1,0},{2,1},{3,2},{5,4},{6,5},{7,6},{9,8},{10,9},{11,10},{13,12},{... | collective-permute-start | bytes 98312 | tf_op jit(solution)/shard_map/ppermute | solution.py:183
  25.9 0.7 copy-start.3
  27.1 8.0 %collective-permute-start.1 = (bf16[256,128]{1,0:T(8,128)(2,1)S(1)}, bf16[256,128]{1,0:T(8,128)(2,1)S(1)}, u32[]{:S(2)}, u32[]{:S(2)}) collective-permute-start(bf16[256,128]{1,0:T(8,128)(2,1)S(1)} %pad_maximum_fusion.1), channel_id=1, source_target_pairs={{0,1},{1,2},{2,3},{4,5},{5,6},{6,7},{8,9},{9,10},{10,11},{12,13},{... | collective-permute-start | bytes 196616 | tf_op jit(solution)/shard_map/ppermute | solution.py:183
  44.7 28.5 %copy-start.2 = (bf16[1,512,512]{2,1,0:T(8,128)(2,1)S(1)}, bf16[1,512,512]{2,1,0:T(8,128)(2,1)}, u32[]{:S(2)}) copy-start(bf16[1,512,512]{2,1,0:T(8,128)(2,1)} %param.5) | copy-start | bytes 1572868

commit v3 on v2

--- a/solution.py
+++ b/solution.py
@@ -210,13 +210,11 @@
     last = orbitals - interface
     inv_root = 1.0 / math.sqrt(orbitals)
     coupling = coupling_matrix(couple_cols[0], couple_vals[0])
-    behind = from_behind(jnp.concatenate([corners[last:, last:], coupling], axis=0), "slab", 1)
-    prev_corner, previous = behind[:interface], behind[interface:]
     next_corner = from_behind(corners[:interface, :interface], "slab", -1)
+    near_prev = dot(coupling.T, corners[last:, last:]).astype(b16)
+    left_part = from_behind((dot(near_prev, coupling) * inv_root).astype(b16), "slab", 1)
     near_next = dot(coupling, next_corner).astype(b16)
-    near_prev = dot(previous.T, prev_corner).astype(b16)
     right_part = dot(near_next, coupling.T) * inv_root
-    left_part = dot(near_prev, previous) * inv_root
     entries, ahead, back, own, right_part, left_part = lax.optimization_barrier(
         (entries, ahead, back, own, right_part, left_part)
     )

time: 133 us -> 133 us (level)
  no operation moved by 1% of the time
where the time goes in v3:
time: 133 us
  blocking collectives  84.1 us (63%)
  starting transfers between devices  26.5 us (20%)
  waiting for transfers between devices  12.7 us (10%)
  Pallas kernels  5.36 us (4%)
  local copies, waits for them, and re-layouts  2.34 us (2%)
    all_to_all x3, blocking collectives, exchange(): return lax.all_to_all(x, 'energy', split_axis=0, concat_axis=0, tiled=True)  84.1 us
    all_to_all x1, starting transfers between devices, exchange(): return lax.all_to_all(x, 'energy', split_axis=0, concat_axis=0, tiled=True)  20.9 us
    all_to_all x1, waiting for transfers between devices, exchange(): return lax.all_to_all(x, 'energy', split_axis=0, concat_axis=0, tiled=True)  8.68 us
    ppermute x2, starting transfers between devices, from_behind(): return lax.ppermute(x, axis, pairs)  5.56 us
    ppermute x2, waiting for transfers between devices, from_behind(): return lax.ppermute(x, axis, pairs)  4 us
  transfers between devices with their start and end apart: 3, of which 2 were waited for; matrix products, arithmetic and copies ran while one was open for 1% of the time, Pallas kernels for 0%

profile of v3, /device:TPU:1, one launch (start us, length us, event | category | flops | bytes accessed | tf_op | source)
XLA Modules:
  0.0 132.8 jit_solution(10988423908791956842)
XLA Ops:
  0.0 1.0 copy-done
  1.0 1.0 shard_map.46
  2.0 20.9 %all-to-all-start = ((bf16[128,16,128]{2,1,0:T(8,128)(2,1)}), bf16[128,16,128]{2,1,0:T(8,128)(2,1)S(1)}, u32[]{:S(2)}, u32[]{:S(2)}) async-start(bf16[128,16,128]{2,1,0:T(8,128)(2,1)} %shard_map.46), calls=%async_computation | async-start | bytes 1048576 | tf_op jit(solution)/shard_map/all_to_all | solution.py:187
  23.0 2.9 %collective-permute-start = (bf16[128,128]{1,0:T(8,128)(2,1)S(1)}, bf16[128,128]{1,0:T(8,128)(2,1)S(1)}, u32[]{:S(2)}, u32[]{:S(2)}) collective-permute-start(bf16[128,128]{1,0:T(8,128)(2,1)S(1)} %slice.6), channel_id=1, source_target_pairs={{1,0},{2,1},{3,2},{5,4},{6,5},{7,6},{9,8},{10,9},{11,10},{13,12},{... | collective-permute-start | bytes 98312 | tf_op jit(solution)/shard_map/ppermute | solution.py:183
  25.9 0.1 copy.8
  26.0 0.6 copy-done.3
  26.7 0.4 select_reduce_fusion
  27.0 0.3 fusion
  27.4 2.7 %collective-permute-start.1 = (bf16[128,128]{1,0:T(8,128)(2,1)S(1)}, bf16[128,128]{1,0:T(8,128)(2,1)S(1)}, u32[]{:S(2)}, u32[]{:S(2)}) collective-permute-start(bf16[128,128]{1,0:T(8,128)(2,1)S(1)} %fusion), channel_id=1, source_target_pairs={{0,1},{1,2},{2,3},{4,5},{5,6},{6,7},{8,9},{9,10},{10,11},{12,13},{... | collective-permute-start | bytes 98312 | tf_op jit(solution)/shard_map/ppermute | solution.py:183
  30.1 0.6 fusion.5
  30.8 4.0 %collective-permute-done = bf16[128,128]{1,0:T(8,128)(2,1)S(1)} collective-permute-done((bf16[128,128]{1,0:T(8,128)(2,1)S(1)}, bf16[128,128]{1,0:T(8,128)(2,1)S(1)}, u32[]{:S(2)}, u32[]{:S(2)}) %collective-permute-start) | collective-permute-done | bytes 32800 | tf_op jit(solution)/shard_map/ppermute | solution.py:183
  34.8 0.3 convolution_multiply_fusion.1.right_ref
  35.0 8.7 %all-to-all-done = bf16[128,16,128]{2,1,0:T(8,128)(2,1)S(1)} async-done(((bf16[128,16,128]{2,1,0:T(8,128)(2,1)}), bf16[128,16,128]{2,1,0:T(8,128)(2,1)S(1)}, u32[]{:S(2)}, u32[]{:S(2)}) %all-to-all-start) | async-done | bytes 524320 | tf_op jit(solution)/shard_map/all_to_all | solution.py:187
  43.7 0.1 copy.16
  43.9 0.8 shard_map.47
  44.6 0.1 copy.10
  44.8 28.4 %all_to_all.20.polar_ref = bf16[128,16,128]{2,1,0:T(8,128)(2,1)S(1)} all-to-all(bf16[128,16,128]{2,1,0:T(8,128)(2,1)S(1)} %bitcast.34), channel_id=1, replica_groups=mesh['energy'=128,'slab'=4] {'energy'}, dimensions={0} | all-to-all | bytes 1048576 | tf_op jit(solution)/shard_map/all_to_all | solution.py:187
  73.2 1.3 shard_map.48
  74.4 28.0 %all_to_all.21 = bf16[128,16,128]{2,1,0:T(8,128)(2,1)S(1)} all-to-all(bf16[128,16,128]{2,1,0:T(8,128)(2,1)S(1)} %shard_map.48), channel_id=1, replica_groups=mesh['energy'=128,'slab'=4] {'energy'}, dimensions={0} | all-to-all | bytes 1048576 | tf_op jit(solution)/shard_map/all_to_all | solution.py:187
  102.5 0.1 copy.15
  102.6 0.7 shard_map.49
  103.3 0.1 copy.12
  103.5 27.7 %all_to_all.22.sigma_ref = bf16[128,16,128]{2,1,0:T(8,128)(2,1)S(1)} all-to-all(bf16[128,16,128]{2,1,0:T(8,128)(2,1)S(1)} %bitcast.36), channel_id=1, replica_groups=mesh['energy'=128,'slab'=4] {'energy'}, dimensions={0} | all-to-all | bytes 1048576 | tf_op jit(solution)/shard_map/all_to_all | solution.py:187
  131.2 1.6 %shard_map.50 = bf16[512,512]{1,0:T(8,128)(2,1)} custom-call(bf16[128,16,128]{2,1,0:T(8,128)(2,1)S(1)} %all_to_all.22.sigma_ref, bf16[512,512]{1,0:T(8,128)(2,1)S(1)} %bitcast.27, f32[128,128]{1,0:T(8,128)S(1)} %convolution_multiply_fusion.1.right_ref, bf16[128,128]{1,0:T(8,128)(2,1)S(1)} %collective-permute-done.1.left_ref), custom_call_target="tpu_custom_call" | custom-call | tf_op jit(solution)/shard_map/pallas_call | solution.py:241
  (18 shorter events, 0.2 us)
Async XLA Ops:
  0.0 1.0 copy-start
  2.0 21.0 %copy-start.1 = (bf16[1,1,512,512]{3,2,1,0:T(8,128)(2,1)S(1)}, bf16[1,1,512,512]{3,2,1,0:T(8,128)(2,1)}, u32[]{:S(2)}) copy-start(bf16[1,1,512,512]{3,2,1,0:T(8,128)(2,1)} %param.4) | copy-start | bytes 1572868
  2.0 41.7 %all-to-all-start = ((bf16[128,16,128]{2,1,0:T(8,128)(2,1)}), bf16[128,16,128]{2,1,0:T(8,128)(2,1)S(1)}, u32[]{:S(2)}, u32[]{:S(2)}) async-start(bf16[128,16,128]{2,1,0:T(8,128)(2,1)} %shard_map.46), calls=%async_computation | async-start | bytes 1048576 | tf_op jit(solution)/shard_map/all_to_all | solution.py:187
  23.0 2.9 %copy-start.4 = (bf16[1,128,8]{1,2,0:T(8,128)(2,1)S(1)}, bf16[1,128,8]{1,2,0:T(8,128)(2,1)}, u32[]{:S(2)}) copy-start(bf16[1,128,8]{1,2,0:T(8,128)(2,1)} %param.7) | copy-start | bytes 6148
  23.0 11.8 %collective-permute-start = (bf16[128,128]{1,0:T(8,128)(2,1)S(1)}, bf16[128,128]{1,0:T(8,128)(2,1)S(1)}, u32[]{:S(2)}, u32[]{:S(2)}) collective-permute-start(bf16[128,128]{1,0:T(8,128)(2,1)S(1)} %slice.6), channel_id=1, source_target_pairs={{1,0},{2,1},{3,2},{5,4},{6,5},{7,6},{9,8},{10,9},{11,10},{13,12},{... | collective-permute-start | bytes 98312 | tf_op jit(solution)/shard_map/ppermute | solution.py:183
  25.9 0.7 copy-start.3
  27.4 7.7 %collective-permute-start.1 = (bf16[128,128]{1,0:T(8,128)(2,1)S(1)}, bf16[128,128]{1,0:T(8,128)(2,1)S(1)}, u32[]{:S(2)}, u32[]{:S(2)}) collective-permute-start(bf16[128,128]{1,0:T(8,128)(2,1)S(1)} %fusion), channel_id=1, source_target_pairs={{0,1},{1,2},{2,3},{4,5},{5,6},{6,7},{8,9},{9,10},{10,11},{12,13},{... | collective-permute-start | bytes 98312 | tf_op jit(solution)/shard_map/ppermute | solution.py:183
  44.8 28.4 %copy-start.2 = (bf16[1,512,512]{2,1,0:T(8,128)(2,1)S(1)}, bf16[1,512,512]{2,1,0:T(8,128)(2,1)}, u32[]{:S(2)}) copy-start(bf16[1,512,512]{2,1,0:T(8,128)(2,1)} %param.5) | copy-start | bytes 1572868

commit v4 on v2

--- a/solution.py
+++ b/solution.py
@@ -72,6 +72,11 @@
     pack(lambda a, b: green_ref[at(a, b)].astype(jnp.float32), blocks, out_ref)
 
 
+def flattened(entries_ref):
+    energies, rows, width = entries_ref.shape
+    return entries_ref[...].reshape(energies, rows * width)
+
+
 def forward(table_ref, entries):
     return dot(table_ref[...], entries)
 
@@ -82,20 +87,24 @@
 
 
 def polar_kernel(scale, entries_ref, own_ref, forward_ref, backward_ref, spectrum_ref, out_ref):
-    spectrum = forward(forward_ref, entries_ref[...])
+    spectrum = forward(forward_ref, flattened(entries_ref))
     spectrum_ref[...] = spectrum
     half, width = spectrum.shape[0] // 2, spectrum.shape[1] // 2
     edge = lax.broadcasted_iota(jnp.int32, (half, width), 0) == 0
     own = own_ref[...] > 0.5
     real = spectrum[:half, :width], spectrum[:half, width:]
     imag = spectrum[half:, :width], spectrum[half:, width:]
+    values = []
     for slot in range(2):
         mirror_real = jnp.where(own, real[slot], real[1 - slot])
         mirror_imag = jnp.where(own, imag[slot], imag[1 - slot])
         rr, ii = real[slot] * mirror_real, imag[slot] * mirror_imag
         ir, ri = imag[slot] * mirror_real, real[slot] * mirror_imag
-        values = backward(backward_ref, jnp.where(edge, rr, rr + ii), jnp.where(edge, ii, ir - ri))
-        out_ref[:, slot * width : (slot + 1) * width] = (values * scale).astype(jnp.bfloat16)
+        values.append(
+            backward(backward_ref, jnp.where(edge, rr, rr + ii), jnp.where(edge, ii, ir - ri))
+        )
+    both = (jnp.concatenate(values, axis=1) * scale).astype(jnp.bfloat16)
+    out_ref[...] = both.reshape(out_ref.shape)
 
 
 def screen_kernel(blocks, polar_ref, coulomb_ref, out_ref, matrix_ref, screened_ref):
@@ -113,7 +122,7 @@
 
 
 def sigma_kernel(scale, entries_ref, green_ref, forward_ref, backward_ref, out_ref):
-    spectrum = forward(forward_ref, entries_ref[...])
+    spectrum = forward(forward_ref, flattened(entries_ref))
     half = spectrum.shape[0] // 2
     edge = lax.broadcasted_iota(jnp.int32, (half, spectrum.shape[1]), 0) == 0
     real, imag = spectrum[:half], spectrum[half:]
@@ -121,7 +130,7 @@
     rr, ii = green_real * real, green_imag * imag
     cross = green_real * imag + green_imag * real
     values = backward(backward_ref, jnp.where(edge, rr, rr - ii), jnp.where(edge, ii, cross))
-    out_ref[...] = (values * scale).astype(jnp.bfloat16)
+    out_ref[...] = (values * scale).astype(jnp.bfloat16).reshape(out_ref.shape)
 
 
 def final_kernel(blocks, inv_root, sigma_ref, green_ref, right_ref, left_ref, out_ref, total_ref):
@@ -223,22 +232,22 @@
 
     spectrum, polar = call(
         functools.partial(polar_kernel, 0.5 / math.sqrt(orbitals * energies)),
-        (jax.ShapeDtypeStruct(flat, f32), jax.ShapeDtypeStruct(flat, b16)),
-    )(entries.reshape(flat), own, ahead, back)
-    polar = exchange(polar.reshape(chunk))
+        (jax.ShapeDtypeStruct(flat, f32), jax.ShapeDtypeStruct(chunk, b16)),
+    )(entries, own, ahead, back)
+    polar = exchange(polar)
 
     screened = call(
         functools.partial(screen_kernel, blocks),
         jax.ShapeDtypeStruct(chunk, b16),
         (pltpu.VMEM((orbitals, orbitals), b16), pltpu.VMEM((orbitals, orbitals), f32)),
     )(polar, coulomb_block)
-    screened = exchange(screened).reshape(flat)
+    screened = exchange(screened)
 
     sigma = call(
         functools.partial(sigma_kernel, 0.2 / math.sqrt(energies)),
-        jax.ShapeDtypeStruct(flat, b16),
+        jax.ShapeDtypeStruct(chunk, b16),
     )(screened, spectrum, ahead, back)
-    sigma = exchange(sigma.reshape(chunk))
+    sigma = exchange(sigma)
 
     updated = call(
         functools.partial(final_kernel, blocks, inv_root),

time: 133 us -> 133 us (level)
  no operation moved by 1% of the time
where the time goes in v4:
time: 133 us; the launch traced here: 132 us
  blocking collectives  84 us (63%)
  starting transfers between devices  26.5 us (20%)
  waiting for transfers between devices  12.6 us (9%)
  Pallas kernels  5.38 us (4%)
  local copies, waits for them, and re-layouts  1.85 us (1%)
    all_to_all x3, blocking collectives, exchange(): return lax.all_to_all(x, 'energy', split_axis=0, concat_axis=0, tiled=True)  84 us
    all_to_all x1, starting transfers between devices, exchange(): return lax.all_to_all(x, 'energy', split_axis=0, concat_axis=0, tiled=True)  20.9 us
    all_to_all x1, waiting for transfers between devices, exchange(): return lax.all_to_all(x, 'energy', split_axis=0, concat_axis=0, tiled=True)  8.33 us
    ppermute x2, starting transfers between devices, from_behind(): return lax.ppermute(x, axis, pairs)  5.56 us
    ppermute x2, waiting for transfers between devices, from_behind(): return lax.ppermute(x, axis, pairs)  4.3 us
  transfers between devices with their start and end apart: 3, of which 2 were waited for; matrix products, arithmetic and copies ran while one was open for 1% of the time, Pallas kernels for 0%

profile of v4, /device:TPU:1, one launch (start us, length us, event | category | flops | bytes accessed | tf_op | source)
XLA Modules:
  0.0 132.1 jit_solution(9448257087047008201)
XLA Ops:
  0.0 1.0 copy-done
  1.0 1.0 shard_map.46
  2.0 20.9 %all-to-all-start = ((bf16[128,16,128]{2,1,0:T(8,128)(2,1)}), bf16[128,16,128]{2,1,0:T(8,128)(2,1)S(1)}, u32[]{:S(2)}, u32[]{:S(2)}) async-start(bf16[128,16,128]{2,1,0:T(8,128)(2,1)} %shard_map.46), calls=%async_computation | async-start | bytes 1048576 | tf_op jit(solution)/shard_map/all_to_all | solution.py:196
  23.0 0.0 copy-start.4
  23.0 2.9 %collective-permute-start = (bf16[128,128]{1,0:T(8,128)(2,1)S(1)}, bf16[128,128]{1,0:T(8,128)(2,1)S(1)}, u32[]{:S(2)}, u32[]{:S(2)}) collective-permute-start(bf16[128,128]{1,0:T(8,128)(2,1)S(1)} %get-tuple-element.26), channel_id=1, source_target_pairs={{1,0},{2,1},{3,2},{5,4},{6,5},{7,6},{9,8},{10,9},{11,10},{13,12},{... | collective-permute-start | bytes 98312 | tf_op jit(solution)/shard_map/ppermute | solution.py:192
  25.9 0.0 copy-start.3
  25.9 0.1 copy.8
  26.0 0.6 copy-done.3
  26.6 0.1 copy.7
  26.7 0.4 select_reduce_fusion
  27.1 2.7 %collective-permute-start.1 = (bf16[256,128]{1,0:T(8,128)(2,1)S(1)}, bf16[256,128]{1,0:T(8,128)(2,1)S(1)}, u32[]{:S(2)}, u32[]{:S(2)}) collective-permute-start(bf16[256,128]{1,0:T(8,128)(2,1)S(1)} %pad_maximum_fusion.1), channel_id=1, source_target_pairs={{0,1},{1,2},{2,3},{4,5},{5,6},{6,7},{8,9},{9,10},{10,11},{12,13},{... | collective-permute-start | bytes 196616 | tf_op jit(solution)/shard_map/ppermute | solution.py:192
  29.8 0.6 fusion.4
  30.5 4.3 %collective-permute-done = bf16[128,128]{1,0:T(8,128)(2,1)S(1)} collective-permute-done((bf16[128,128]{1,0:T(8,128)(2,1)S(1)}, bf16[128,128]{1,0:T(8,128)(2,1)S(1)}, u32[]{:S(2)}, u32[]{:S(2)}) %collective-permute-start) | collective-permute-done | bytes 32800 | tf_op jit(solution)/shard_map/ppermute | solution.py:192
  34.8 0.3 convolution_multiply_fusion.1.right_ref
  35.0 0.3 convolution_multiply_fusion.left_ref
  35.3 8.3 %all-to-all-done.entries_ref = bf16[128,16,128]{2,1,0:T(8,128)(2,1)S(1)} async-done(((bf16[128,16,128]{2,1,0:T(8,128)(2,1)}), bf16[128,16,128]{2,1,0:T(8,128)(2,1)S(1)}, u32[]{:S(2)}, u32[]{:S(2)}) %all-to-all-start) | async-done | bytes 524320 | tf_op jit(solution)/shard_map/all_to_all | solution.py:196
  43.7 0.8 shard_map.47
  44.5 0.0 copy-start.2
  44.5 28.4 %all_to_all.20.polar_ref = bf16[128,16,128]{2,1,0:T(8,128)(2,1)S(1)} all-to-all(bf16[128,16,128]{2,1,0:T(8,128)(2,1)S(1)} %get-tuple-element.21), channel_id=1, replica_groups=mesh['energy'=128,'slab'=4] {'energy'}, dimensions={0} | all-to-all | bytes 1048576 | tf_op jit(solution)/shard_map/all_to_all | solution.py:196
  72.9 1.3 shard_map.48
  74.2 28.1 %all_to_all.21.entries_ref = bf16[128,16,128]{2,1,0:T(8,128)(2,1)S(1)} all-to-all(bf16[128,16,128]{2,1,0:T(8,128)(2,1)S(1)} %shard_map.48), channel_id=1, replica_groups=mesh['energy'=128,'slab'=4] {'energy'}, dimensions={0} | all-to-all | bytes 1048576 | tf_op jit(solution)/shard_map/all_to_all | solution.py:196
  102.3 0.7 shard_map.49
  103.0 27.5 %all_to_all.22.sigma_ref = bf16[128,16,128]{2,1,0:T(8,128)(2,1)S(1)} all-to-all(bf16[128,16,128]{2,1,0:T(8,128)(2,1)S(1)} %shard_map.49), channel_id=1, replica_groups=mesh['energy'=128,'slab'=4] {'energy'}, dimensions={0} | all-to-all | bytes 1048576 | tf_op jit(solution)/shard_map/all_to_all | solution.py:196
  130.5 1.6 %shard_map.50 = bf16[512,512]{1,0:T(8,128)(2,1)} custom-call(bf16[128,16,128]{2,1,0:T(8,128)(2,1)S(1)} %all_to_all.22.sigma_ref, bf16[512,512]{1,0:T(8,128)(2,1)S(1)} %bitcast.12, f32[128,128]{1,0:T(8,128)S(1)} %convolution_multiply_fusion.1.right_ref, f32[128,128]{1,0:T(8,128)S(1)} %convolution_multiply_fusion.left_ref), custom_call_target="tpu_custom_call" | custom-call | tf_op jit(solution)/shard_map/pallas_call | solution.py:252
  (15 shorter events, 0.1 us)
Async XLA Ops:
  0.0 1.0 copy-start
  2.0 21.0 %copy-start.1 = (bf16[1,1,512,512]{3,2,1,0:T(8,128)(2,1)S(1)}, bf16[1,1,512,512]{3,2,1,0:T(8,128)(2,1)}, u32[]{:S(2)}) copy-start(bf16[1,1,512,512]{3,2,1,0:T(8,128)(2,1)} %param.4) | copy-start | bytes 1572868
  2.0 41.7 %all-to-all-start = ((bf16[128,16,128]{2,1,0:T(8,128)(2,1)}), bf16[128,16,128]{2,1,0:T(8,128)(2,1)S(1)}, u32[]{:S(2)}, u32[]{:S(2)}) async-start(bf16[128,16,128]{2,1,0:T(8,128)(2,1)} %shard_map.46), calls=%async_computation | async-start | bytes 1048576 | tf_op jit(solution)/shard_map/all_to_all | solution.py:196
  23.0 2.9 %copy-start.4 = (bf16[1,128,8]{1,2,0:T(8,128)(2,1)S(1)}, bf16[1,128,8]{1,2,0:T(8,128)(2,1)}, u32[]{:S(2)}) copy-start(bf16[1,128,8]{1,2,0:T(8,128)(2,1)} %param.7) | copy-start | bytes 6148
  23.0 11.8 %collective-permute-start = (bf16[128,128]{1,0:T(8,128)(2,1)S(1)}, bf16[128,128]{1,0:T(8,128)(2,1)S(1)}, u32[]{:S(2)}, u32[]{:S(2)}) collective-permute-start(bf16[128,128]{1,0:T(8,128)(2,1)S(1)} %get-tuple-element.26), channel_id=1, source_target_pairs={{1,0},{2,1},{3,2},{5,4},{6,5},{7,6},{9,8},{10,9},{11,10},{13,12},{... | collective-permute-start | bytes 98312 | tf_op jit(solution)/shard_map/ppermute | solution.py:192
  25.9 0.7 copy-start.3
  27.1 8.0 %collective-permute-start.1 = (bf16[256,128]{1,0:T(8,128)(2,1)S(1)}, bf16[256,128]{1,0:T(8,128)(2,1)S(1)}, u32[]{:S(2)}, u32[]{:S(2)}) collective-permute-start(bf16[256,128]{1,0:T(8,128)(2,1)S(1)} %pad_maximum_fusion.1), channel_id=1, source_target_pairs={{0,1},{1,2},{2,3},{4,5},{5,6},{6,7},{8,9},{9,10},{10,11},{12,13},{... | collective-permute-start | bytes 196616 | tf_op jit(solution)/shard_map/ppermute | solution.py:192
  44.5 28.5 %copy-start.2 = (bf16[1,512,512]{2,1,0:T(8,128)(2,1)S(1)}, bf16[1,512,512]{2,1,0:T(8,128)(2,1)}, u32[]{:S(2)}) copy-start(bf16[1,512,512]{2,1,0:T(8,128)(2,1)} %param.5) | copy-start | bytes 1572868

commit v5 on v4

--- a/solution.py
+++ b/solution.py
@@ -133,17 +133,20 @@
     out_ref[...] = (values * scale).astype(jnp.bfloat16).reshape(out_ref.shape)
 
 
-def final_kernel(blocks, inv_root, sigma_ref, green_ref, right_ref, left_ref, out_ref, total_ref):
+def final_kernel(blocks, inv_root, sigma_ref, green_ref, right_ref, left_ref, out_ref):
+    total = [[None] * blocks for _ in range(blocks)]
+
     def store(a, b, value):
         if a == b == blocks - 1:
             value = value + right_ref[...]
         if a == b == 0:
             value = value + left_ref[...]
-        total_ref[at(a, b)] = value.astype(jnp.bfloat16)
+        total[a][b] = value.astype(jnp.bfloat16)
 
     unpack(sigma_ref, blocks, store)
     green = green_ref[...]
-    dressed = dot(green, total_ref[...]).astype(jnp.bfloat16)
+    whole = jnp.concatenate([jnp.concatenate(row, axis=1) for row in total], axis=0)
+    dressed = dot(green, whole).astype(jnp.bfloat16)
     updated = green.astype(jnp.float32) + dot(dressed, green) * inv_root
     out_ref[...] = updated.astype(jnp.bfloat16)
 
@@ -252,7 +255,6 @@
     updated = call(
         functools.partial(final_kernel, blocks, inv_root),
         jax.ShapeDtypeStruct((orbitals, orbitals), b16),
-        (pltpu.VMEM((orbitals, orbitals), b16),),
     )(sigma, green, right_part, left_part)
     return updated[None, None]
 

time: 133 us -> 132 us (level)
  no operation moved by 1% of the time
where the time goes in v5:
time: 132 us
  blocking collectives  84 us (64%)
  starting transfers between devices  26.5 us (20%)
  waiting for transfers between devices  12.6 us (10%)
  Pallas kernels  5.32 us (4%)
  local copies, waits for them, and re-layouts  1.85 us (1%)
    all_to_all x3, blocking collectives, exchange(): return lax.all_to_all(x, 'energy', split_axis=0, concat_axis=0, tiled=True)  84 us
    all_to_all x1, starting transfers between devices, exchange(): return lax.all_to_all(x, 'energy', split_axis=0, concat_axis=0, tiled=True)  20.9 us
    all_to_all x1, waiting for transfers between devices, exchange(): return lax.all_to_all(x, 'energy', split_axis=0, concat_axis=0, tiled=True)  8.33 us
    ppermute x2, starting transfers between devices, from_behind(): return lax.ppermute(x, axis, pairs)  5.56 us
    ppermute x2, waiting for transfers between devices, from_behind(): return lax.ppermute(x, axis, pairs)  4.3 us
  transfers between devices with their start and end apart: 3, of which 2 were waited for; matrix products, arithmetic and copies ran while one was open for 1% of the time, Pallas kernels for 0%

profile of v5, /device:TPU:1, one launch (start us, length us, event | category | flops | bytes accessed | tf_op | source)
XLA Modules:
  0.0 132.1 jit_solution(1681463579318763975)
XLA Ops:
  0.0 1.0 copy-done
  1.0 1.0 shard_map.46
  2.0 20.9 %all-to-all-start = ((bf16[128,16,128]{2,1,0:T(8,128)(2,1)}), bf16[128,16,128]{2,1,0:T(8,128)(2,1)S(1)}, u32[]{:S(2)}, u32[]{:S(2)}) async-start(bf16[128,16,128]{2,1,0:T(8,128)(2,1)} %shard_map.46), calls=%async_computation | async-start | bytes 1048576 | tf_op jit(solution)/shard_map/all_to_all | solution.py:199
  23.0 0.0 copy-start.4
  23.0 2.9 %collective-permute-start = (bf16[128,128]{1,0:T(8,128)(2,1)S(1)}, bf16[128,128]{1,0:T(8,128)(2,1)S(1)}, u32[]{:S(2)}, u32[]{:S(2)}) collective-permute-start(bf16[128,128]{1,0:T(8,128)(2,1)S(1)} %get-tuple-element.26), channel_id=1, source_target_pairs={{1,0},{2,1},{3,2},{5,4},{6,5},{7,6},{9,8},{10,9},{11,10},{13,12},{... | collective-permute-start | bytes 98312 | tf_op jit(solution)/shard_map/ppermute | solution.py:195
  25.9 0.0 copy-start.3
  25.9 0.1 copy.8
  26.0 0.6 copy-done.3
  26.6 0.1 copy.7
  26.7 0.4 select_reduce_fusion
  27.1 2.7 %collective-permute-start.1 = (bf16[256,128]{1,0:T(8,128)(2,1)S(1)}, bf16[256,128]{1,0:T(8,128)(2,1)S(1)}, u32[]{:S(2)}, u32[]{:S(2)}) collective-permute-start(bf16[256,128]{1,0:T(8,128)(2,1)S(1)} %pad_maximum_fusion.1), channel_id=1, source_target_pairs={{0,1},{1,2},{2,3},{4,5},{5,6},{6,7},{8,9},{9,10},{10,11},{12,13},{... | collective-permute-start | bytes 196616 | tf_op jit(solution)/shard_map/ppermute | solution.py:195
  29.8 0.6 fusion.4
  30.5 4.3 %collective-permute-done = bf16[128,128]{1,0:T(8,128)(2,1)S(1)} collective-permute-done((bf16[128,128]{1,0:T(8,128)(2,1)S(1)}, bf16[128,128]{1,0:T(8,128)(2,1)S(1)}, u32[]{:S(2)}, u32[]{:S(2)}) %collective-permute-start) | collective-permute-done | bytes 32800 | tf_op jit(solution)/shard_map/ppermute | solution.py:195
  34.8 0.3 convolution_multiply_fusion.1.right_ref
  35.0 0.3 convolution_multiply_fusion.left_ref
  35.3 8.3 %all-to-all-done.entries_ref = bf16[128,16,128]{2,1,0:T(8,128)(2,1)S(1)} async-done(((bf16[128,16,128]{2,1,0:T(8,128)(2,1)}), bf16[128,16,128]{2,1,0:T(8,128)(2,1)S(1)}, u32[]{:S(2)}, u32[]{:S(2)}) %all-to-all-start) | async-done | bytes 524320 | tf_op jit(solution)/shard_map/all_to_all | solution.py:199
  43.7 0.8 shard_map.47
  44.5 0.0 copy-start.2
  44.5 28.4 %all_to_all.20.polar_ref = bf16[128,16,128]{2,1,0:T(8,128)(2,1)S(1)} all-to-all(bf16[128,16,128]{2,1,0:T(8,128)(2,1)S(1)} %get-tuple-element.21), channel_id=1, replica_groups=mesh['energy'=128,'slab'=4] {'energy'}, dimensions={0} | all-to-all | bytes 1048576 | tf_op jit(solution)/shard_map/all_to_all | solution.py:199
  72.9 1.3 shard_map.48
  74.2 28.1 %all_to_all.21.entries_ref = bf16[128,16,128]{2,1,0:T(8,128)(2,1)S(1)} all-to-all(bf16[128,16,128]{2,1,0:T(8,128)(2,1)S(1)} %shard_map.48), channel_id=1, replica_groups=mesh['energy'=128,'slab'=4] {'energy'}, dimensions={0} | all-to-all | bytes 1048576 | tf_op jit(solution)/shard_map/all_to_all | solution.py:199
  102.3 0.7 shard_map.49
  103.0 27.5 %all_to_all.22.sigma_ref = bf16[128,16,128]{2,1,0:T(8,128)(2,1)S(1)} all-to-all(bf16[128,16,128]{2,1,0:T(8,128)(2,1)S(1)} %shard_map.49), channel_id=1, replica_groups=mesh['energy'=128,'slab'=4] {'energy'}, dimensions={0} | all-to-all | bytes 1048576 | tf_op jit(solution)/shard_map/all_to_all | solution.py:199
  130.5 1.6 %shard_map.50 = bf16[512,512]{1,0:T(8,128)(2,1)} custom-call(bf16[128,16,128]{2,1,0:T(8,128)(2,1)S(1)} %all_to_all.22.sigma_ref, bf16[512,512]{1,0:T(8,128)(2,1)S(1)} %bitcast.12, f32[128,128]{1,0:T(8,128)S(1)} %convolution_multiply_fusion.1.right_ref, f32[128,128]{1,0:T(8,128)S(1)} %convolution_multiply_fusion.left_ref), custom_call_target="tpu_custom_call" | custom-call | tf_op jit(solution)/shard_map/pallas_call | solution.py:255
  (15 shorter events, 0.1 us)
Async XLA Ops:
  0.0 1.0 copy-start
  2.0 21.0 %copy-start.1 = (bf16[1,1,512,512]{3,2,1,0:T(8,128)(2,1)S(1)}, bf16[1,1,512,512]{3,2,1,0:T(8,128)(2,1)}, u32[]{:S(2)}) copy-start(bf16[1,1,512,512]{3,2,1,0:T(8,128)(2,1)} %param.4) | copy-start | bytes 1572868
  2.0 41.7 %all-to-all-start = ((bf16[128,16,128]{2,1,0:T(8,128)(2,1)}), bf16[128,16,128]{2,1,0:T(8,128)(2,1)S(1)}, u32[]{:S(2)}, u32[]{:S(2)}) async-start(bf16[128,16,128]{2,1,0:T(8,128)(2,1)} %shard_map.46), calls=%async_computation | async-start | bytes 1048576 | tf_op jit(solution)/shard_map/all_to_all | solution.py:199
  23.0 2.9 %copy-start.4 = (bf16[1,128,8]{1,2,0:T(8,128)(2,1)S(1)}, bf16[1,128,8]{1,2,0:T(8,128)(2,1)}, u32[]{:S(2)}) copy-start(bf16[1,128,8]{1,2,0:T(8,128)(2,1)} %param.7) | copy-start | bytes 6148
  23.0 11.8 %collective-permute-start = (bf16[128,128]{1,0:T(8,128)(2,1)S(1)}, bf16[128,128]{1,0:T(8,128)(2,1)S(1)}, u32[]{:S(2)}, u32[]{:S(2)}) collective-permute-start(bf16[128,128]{1,0:T(8,128)(2,1)S(1)} %get-tuple-element.26), channel_id=1, source_target_pairs={{1,0},{2,1},{3,2},{5,4},{6,5},{7,6},{9,8},{10,9},{11,10},{13,12},{... | collective-permute-start | bytes 98312 | tf_op jit(solution)/shard_map/ppermute | solution.py:195
  25.9 0.7 copy-start.3
  27.1 8.0 %collective-permute-start.1 = (bf16[256,128]{1,0:T(8,128)(2,1)S(1)}, bf16[256,128]{1,0:T(8,128)(2,1)S(1)}, u32[]{:S(2)}, u32[]{:S(2)}) collective-permute-start(bf16[256,128]{1,0:T(8,128)(2,1)S(1)} %pad_maximum_fusion.1), channel_id=1, source_target_pairs={{0,1},{1,2},{2,3},{4,5},{5,6},{6,7},{8,9},{9,10},{10,11},{12,13},{... | collective-permute-start | bytes 196616 | tf_op jit(solution)/shard_map/ppermute | solution.py:195
  44.5 28.5 %copy-start.2 = (bf16[1,512,512]{2,1,0:T(8,128)(2,1)S(1)}, bf16[1,512,512]{2,1,0:T(8,128)(2,1)}, u32[]{:S(2)}) copy-start(bf16[1,512,512]{2,1,0:T(8,128)(2,1)} %param.5) | copy-start | bytes 1572868

commit v6 on v5

--- a/solution.py
+++ b/solution.py
@@ -34,7 +34,7 @@
     return row <= column, row < column
 
 
-def pack(block, blocks, out_ref):
+def pack(block, blocks, out_ref, after=lambda p: None):
     apart, diagonal = pairs_of(blocks)
     upper, above = triangle()
     for p, (a, b) in enumerate(apart + diagonal):
@@ -47,6 +47,7 @@
             [first.reshape(OWNERS, ROWS, BLOCK), second.reshape(OWNERS, ROWS, BLOCK)], axis=1
         )
         out_ref[p * OWNERS : (p + 1) * OWNERS] = both.astype(jnp.bfloat16)
+        after(p)
 
 
 def unpack(in_ref, blocks, store):
@@ -68,8 +69,22 @@
     return pl.ds(a * BLOCK, BLOCK), pl.ds(b * BLOCK, BLOCK)
 
 
-def pack_kernel(blocks, green_ref, out_ref):
-    pack(lambda a, b: green_ref[at(a, b)].astype(jnp.float32), blocks, out_ref)
+def pack_kernel(blocks, green_ref, out_ref, packed_ref, sems):
+    half = packed_ref.shape[0] // 2
+    copies = [
+        pltpu.make_async_copy(
+            packed_ref.at[pl.ds(i * half, half)], out_ref.at[pl.ds(i * half, half)], sems.at[i]
+        )
+        for i in range(2)
+    ]
+
+    def after(p):
+        if (p + 1) * OWNERS % half == 0:
+            copies[p * OWNERS // half].start()
+
+    pack(lambda a, b: green_ref[at(a, b)].astype(jnp.float32), blocks, packed_ref, after)
+    for copy in copies:
+        copy.wait()
 
 
 def flattened(entries_ref):
@@ -151,10 +166,11 @@
     out_ref[...] = updated.astype(jnp.bfloat16)
 
 
-def call(kernel, outs, scratch=(), flops=0, moved=0):
+def call(kernel, outs, scratch=(), flops=0, moved=0, **specs):
     return pl.pallas_call(
         kernel,
         out_shape=outs,
+        **specs,
         scratch_shapes=list(scratch),
         compiler_params=pltpu.CompilerParams(vmem_limit_bytes=LIMIT),
         cost_estimate=pl.CostEstimate(flops=flops, bytes_accessed=moved, transcendentals=0),
@@ -207,7 +223,12 @@
     chunk = (energies, 2 * ROWS, BLOCK)
     flat = (energies, 2 * ROWS * BLOCK)
     f32, b16 = jnp.float32, jnp.bfloat16
-    packed = call(functools.partial(pack_kernel, blocks), jax.ShapeDtypeStruct(chunk, b16))(green)
+    packed = call(
+        functools.partial(pack_kernel, blocks),
+        jax.ShapeDtypeStruct(chunk, b16),
+        (pltpu.VMEM(chunk, b16), pltpu.SemaphoreType.DMA((2,))),
+        out_specs=pl.BlockSpec(memory_space=pltpu.HBM),
+    )(green)
     packed, corners = lax.optimization_barrier((packed, green))
     entries = exchange(packed)
 

time: 132 us -> 133 us (level)
  no operation moved by 1% of the time
where the time goes in v6:
time: 133 us; the launch traced here: 132 us
  blocking collectives  84.2 us (63%)
  starting transfers between devices  26.5 us (20%)
  waiting for transfers between devices  12.6 us (9%)
  Pallas kernels  5.27 us (4%)
  local copies, waits for them, and re-layouts  1.85 us (1%)
    all_to_all x3, blocking collectives, exchange(): return lax.all_to_all(x, 'energy', split_axis=0, concat_axis=0, tiled=True)  84.2 us
    all_to_all x1, starting transfers between devices, exchange(): return lax.all_to_all(x, 'energy', split_axis=0, concat_axis=0, tiled=True)  21 us
    all_to_all x1, waiting for transfers between devices, exchange(): return lax.all_to_all(x, 'energy', split_axis=0, concat_axis=0, tiled=True)  8.33 us
    ppermute x2, starting transfers between devices, from_behind(): return lax.ppermute(x, axis, pairs)  5.56 us
    ppermute x2, waiting for transfers between devices, from_behind(): return lax.ppermute(x, axis, pairs)  4.3 us
  transfers between devices with their start and end apart: 3, of which 2 were waited for; matrix products, arithmetic and copies ran while one was open for 1% of the time, Pallas kernels for 0%

profile of v6, /device:TPU:1, one launch (start us, length us, event | category | flops | bytes accessed | tf_op | source)
XLA Modules:
  0.0 132.3 jit_solution(6702625985611472363)
XLA Ops:
  0.0 1.0 copy-done
  1.0 0.9 shard_map.46
  2.0 0.0 copy-start.1
  2.0 21.0 %all-to-all-start = ((bf16[128,16,128]{2,1,0:T(8,128)(2,1)}), bf16[128,16,128]{2,1,0:T(8,128)(2,1)S(1)}, u32[]{:S(2)}, u32[]{:S(2)}) async-start(bf16[128,16,128]{2,1,0:T(8,128)(2,1)} %shard_map.46), calls=%async_computation | async-start | bytes 1048576 | tf_op jit(solution)/shard_map/all_to_all | solution.py:215
  23.0 0.0 copy-start.4
  23.0 2.9 %collective-permute-start = (bf16[128,128]{1,0:T(8,128)(2,1)S(1)}, bf16[128,128]{1,0:T(8,128)(2,1)S(1)}, u32[]{:S(2)}, u32[]{:S(2)}) collective-permute-start(bf16[128,128]{1,0:T(8,128)(2,1)S(1)} %get-tuple-element.26), channel_id=1, source_target_pairs={{1,0},{2,1},{3,2},{5,4},{6,5},{7,6},{9,8},{10,9},{11,10},{13,12},{... | collective-permute-start | bytes 98312 | tf_op jit(solution)/shard_map/ppermute | solution.py:211
  25.9 0.1 copy.8
  26.0 0.6 copy-done.3
  26.6 0.1 copy.7
  26.7 0.4 select_reduce_fusion
  27.0 2.7 %collective-permute-start.1 = (bf16[256,128]{1,0:T(8,128)(2,1)S(1)}, bf16[256,128]{1,0:T(8,128)(2,1)S(1)}, u32[]{:S(2)}, u32[]{:S(2)}) collective-permute-start(bf16[256,128]{1,0:T(8,128)(2,1)S(1)} %pad_maximum_fusion.1), channel_id=1, source_target_pairs={{0,1},{1,2},{2,3},{4,5},{5,6},{6,7},{8,9},{9,10},{10,11},{12,13},{... | collective-permute-start | bytes 196616 | tf_op jit(solution)/shard_map/ppermute | solution.py:211
  29.8 0.6 fusion.4
  30.4 4.3 %collective-permute-done = bf16[128,128]{1,0:T(8,128)(2,1)S(1)} collective-permute-done((bf16[128,128]{1,0:T(8,128)(2,1)S(1)}, bf16[128,128]{1,0:T(8,128)(2,1)S(1)}, u32[]{:S(2)}, u32[]{:S(2)}) %collective-permute-start) | collective-permute-done | bytes 32800 | tf_op jit(solution)/shard_map/ppermute | solution.py:211
  34.7 0.3 convolution_multiply_fusion.1.right_ref
  35.0 0.3 convolution_multiply_fusion.left_ref
  35.3 8.3 %all-to-all-done.entries_ref = bf16[128,16,128]{2,1,0:T(8,128)(2,1)S(1)} async-done(((bf16[128,16,128]{2,1,0:T(8,128)(2,1)}), bf16[128,16,128]{2,1,0:T(8,128)(2,1)S(1)}, u32[]{:S(2)}, u32[]{:S(2)}) %all-to-all-start) | async-done | bytes 524320 | tf_op jit(solution)/shard_map/all_to_all | solution.py:215
  43.7 0.8 shard_map.47
  44.4 0.0 copy-start.2
  44.4 28.4 %all_to_all.20.polar_ref = bf16[128,16,128]{2,1,0:T(8,128)(2,1)S(1)} all-to-all(bf16[128,16,128]{2,1,0:T(8,128)(2,1)S(1)} %get-tuple-element.21), channel_id=1, replica_groups=mesh['energy'=128,'slab'=4] {'energy'}, dimensions={0} | all-to-all | bytes 1048576 | tf_op jit(solution)/shard_map/all_to_all | solution.py:215
  72.9 1.3 shard_map.48
  74.2 28.0 %all_to_all.21.entries_ref = bf16[128,16,128]{2,1,0:T(8,128)(2,1)S(1)} all-to-all(bf16[128,16,128]{2,1,0:T(8,128)(2,1)S(1)} %shard_map.48), channel_id=1, replica_groups=mesh['energy'=128,'slab'=4] {'energy'}, dimensions={0} | all-to-all | bytes 1048576 | tf_op jit(solution)/shard_map/all_to_all | solution.py:215
  102.2 0.7 shard_map.49
  103.0 27.7 %all_to_all.22.sigma_ref = bf16[128,16,128]{2,1,0:T(8,128)(2,1)S(1)} all-to-all(bf16[128,16,128]{2,1,0:T(8,128)(2,1)S(1)} %shard_map.49), channel_id=1, replica_groups=mesh['energy'=128,'slab'=4] {'energy'}, dimensions={0} | all-to-all | bytes 1048576 | tf_op jit(solution)/shard_map/all_to_all | solution.py:215
  130.7 1.6 %shard_map.50 = bf16[512,512]{1,0:T(8,128)(2,1)} custom-call(bf16[128,16,128]{2,1,0:T(8,128)(2,1)S(1)} %all_to_all.22.sigma_ref, bf16[512,512]{1,0:T(8,128)(2,1)S(1)} %bitcast.12, f32[128,128]{1,0:T(8,128)S(1)} %convolution_multiply_fusion.1.right_ref, f32[128,128]{1,0:T(8,128)S(1)} %convolution_multiply_fusion.left_ref), custom_call_target="tpu_custom_call" | custom-call | tf_op jit(solution)/shard_map/pallas_call | solution.py:276
  (15 shorter events, 0.1 us)
Async XLA Ops:
  0.0 1.0 copy-start
  2.0 21.0 %copy-start.1 = (bf16[1,1,512,512]{3,2,1,0:T(8,128)(2,1)S(1)}, bf16[1,1,512,512]{3,2,1,0:T(8,128)(2,1)}, u32[]{:S(2)}) copy-start(bf16[1,1,512,512]{3,2,1,0:T(8,128)(2,1)} %param.4) | copy-start | bytes 1572868
  2.0 41.7 %all-to-all-start = ((bf16[128,16,128]{2,1,0:T(8,128)(2,1)}), bf16[128,16,128]{2,1,0:T(8,128)(2,1)S(1)}, u32[]{:S(2)}, u32[]{:S(2)}) async-start(bf16[128,16,128]{2,1,0:T(8,128)(2,1)} %shard_map.46), calls=%async_computation | async-start | bytes 1048576 | tf_op jit(solution)/shard_map/all_to_all | solution.py:215
  23.0 2.9 %copy-start.4 = (bf16[1,128,8]{1,2,0:T(8,128)(2,1)S(1)}, bf16[1,128,8]{1,2,0:T(8,128)(2,1)}, u32[]{:S(2)}) copy-start(bf16[1,128,8]{1,2,0:T(8,128)(2,1)} %param.7) | copy-start | bytes 6148
  23.0 11.8 %collective-permute-start = (bf16[128,128]{1,0:T(8,128)(2,1)S(1)}, bf16[128,128]{1,0:T(8,128)(2,1)S(1)}, u32[]{:S(2)}, u32[]{:S(2)}) collective-permute-start(bf16[128,128]{1,0:T(8,128)(2,1)S(1)} %get-tuple-element.26), channel_id=1, source_target_pairs={{1,0},{2,1},{3,2},{5,4},{6,5},{7,6},{9,8},{10,9},{11,10},{13,12},{... | collective-permute-start | bytes 98312 | tf_op jit(solution)/shard_map/ppermute | solution.py:211
  25.9 0.7 copy-start.3
  27.0 8.0 %collective-permute-start.1 = (bf16[256,128]{1,0:T(8,128)(2,1)S(1)}, bf16[256,128]{1,0:T(8,128)(2,1)S(1)}, u32[]{:S(2)}, u32[]{:S(2)}) collective-permute-start(bf16[256,128]{1,0:T(8,128)(2,1)S(1)} %pad_maximum_fusion.1), channel_id=1, source_target_pairs={{0,1},{1,2},{2,3},{4,5},{5,6},{6,7},{8,9},{9,10},{10,11},{12,13},{... | collective-permute-start | bytes 196616 | tf_op jit(solution)/shard_map/ppermute | solution.py:211
  44.4 28.5 %copy-start.2 = (bf16[1,512,512]{2,1,0:T(8,128)(2,1)S(1)}, bf16[1,512,512]{2,1,0:T(8,128)(2,1)}, u32[]{:S(2)}) copy-start(bf16[1,512,512]{2,1,0:T(8,128)(2,1)} %param.5) | copy-start | bytes 1572868

commit v7 on v5

--- a/solution.py
+++ b/solution.py
@@ -107,18 +107,29 @@
     out_ref[...] = both.reshape(out_ref.shape)
 
 
-def screen_kernel(blocks, polar_ref, coulomb_ref, out_ref, matrix_ref, screened_ref):
+def screen_kernel(blocks, polar_ref, coulomb_ref, out_ref, matrix_ref):
     def store(a, b, value):
         matrix_ref[at(a, b)] = value.astype(jnp.bfloat16)
 
     unpack(polar_ref, blocks, store)
     coulomb = coulomb_ref[...]
     inner = dot(coulomb, matrix_ref[...]).astype(jnp.bfloat16)
-    second = dot(inner, coulomb)
-    third = dot(inner, second.astype(jnp.bfloat16))
-    screened = (coulomb.astype(jnp.float32) + second + third).astype(jnp.bfloat16)
-    screened_ref[...] = screened.astype(jnp.float32)
-    pack(lambda a, b: screened_ref[at(a, b)], blocks, out_ref)
+    half = coulomb.shape[1] // 2
+    sides = [slice(0, half), slice(half, 2 * half)]
+    second = [dot(inner, coulomb_ref[:, side]) for side in sides]
+    rounded = [part.astype(jnp.bfloat16) for part in second]
+    screened = jnp.concatenate(
+        [
+            coulomb_ref[:, side].astype(jnp.float32) + part + dot(inner, low)
+            for side, part, low in zip(sides, second, rounded)
+        ],
+        axis=1,
+    )
+
+    def block(a, b):
+        return screened[a * BLOCK : (a + 1) * BLOCK, b * BLOCK : (b + 1) * BLOCK]
+
+    pack(block, blocks, out_ref)
 
 
 def sigma_kernel(scale, entries_ref, green_ref, forward_ref, backward_ref, out_ref):
@@ -242,7 +253,7 @@
     screened = call(
         functools.partial(screen_kernel, blocks),
         jax.ShapeDtypeStruct(chunk, b16),
-        (pltpu.VMEM((orbitals, orbitals), b16), pltpu.VMEM((orbitals, orbitals), f32)),
+        (pltpu.VMEM((orbitals, orbitals), b16),),
     )(polar, coulomb_block)
     screened = exchange(screened)
 

time: 132 us -> 133 us (level)
  no operation moved by 1% of the time
where the time goes in v7:
time: 133 us; the launch traced here: 132 us
  blocking collectives  84.2 us (63%)
  starting transfers between devices  26.5 us (20%)
  waiting for transfers between devices  12.6 us (9%)
  Pallas kernels  5.3 us (4%)
  local copies, waits for them, and re-layouts  1.85 us (1%)
    all_to_all x3, blocking collectives, exchange(): return lax.all_to_all(x, 'energy', split_axis=0, concat_axis=0, tiled=True)  84.2 us
    all_to_all x1, starting transfers between devices, exchange(): return lax.all_to_all(x, 'energy', split_axis=0, concat_axis=0, tiled=True)  20.9 us
    all_to_all x1, waiting for transfers between devices, exchange(): return lax.all_to_all(x, 'energy', split_axis=0, concat_axis=0, tiled=True)  8.33 us
    ppermute x2, starting transfers between devices, from_behind(): return lax.ppermute(x, axis, pairs)  5.56 us
    ppermute x2, waiting for transfers between devices, from_behind(): return lax.ppermute(x, axis, pairs)  4.3 us
  transfers between devices with their start and end apart: 3, of which 2 were waited for; matrix products, arithmetic and copies ran while one was open for 1% of the time, Pallas kernels for 0%

profile of v7, /device:TPU:1, one launch (start us, length us, event | category | flops | bytes accessed | tf_op | source)
XLA Modules:
  0.0 132.3 jit_solution(3111368153518636277)
XLA Ops:
  0.0 1.0 copy-done
  1.0 1.0 shard_map.46
  2.0 20.9 %all-to-all-start = ((bf16[128,16,128]{2,1,0:T(8,128)(2,1)}), bf16[128,16,128]{2,1,0:T(8,128)(2,1)S(1)}, u32[]{:S(2)}, u32[]{:S(2)}) async-start(bf16[128,16,128]{2,1,0:T(8,128)(2,1)} %shard_map.46), calls=%async_computation | async-start | bytes 1048576 | tf_op jit(solution)/shard_map/all_to_all | solution.py:210
  23.0 0.0 copy-start.4
  23.0 2.9 %collective-permute-start = (bf16[128,128]{1,0:T(8,128)(2,1)S(1)}, bf16[128,128]{1,0:T(8,128)(2,1)S(1)}, u32[]{:S(2)}, u32[]{:S(2)}) collective-permute-start(bf16[128,128]{1,0:T(8,128)(2,1)S(1)} %get-tuple-element.26), channel_id=1, source_target_pairs={{1,0},{2,1},{3,2},{5,4},{6,5},{7,6},{9,8},{10,9},{11,10},{13,12},{... | collective-permute-start | bytes 98312 | tf_op jit(solution)/shard_map/ppermute | solution.py:206
  25.9 0.0 copy-start.3
  25.9 0.1 copy.8
  26.0 0.6 copy-done.3
  26.6 0.1 copy.7
  26.7 0.4 select_reduce_fusion
  27.1 2.7 %collective-permute-start.1 = (bf16[256,128]{1,0:T(8,128)(2,1)S(1)}, bf16[256,128]{1,0:T(8,128)(2,1)S(1)}, u32[]{:S(2)}, u32[]{:S(2)}) collective-permute-start(bf16[256,128]{1,0:T(8,128)(2,1)S(1)} %pad_maximum_fusion.1), channel_id=1, source_target_pairs={{0,1},{1,2},{2,3},{4,5},{5,6},{6,7},{8,9},{9,10},{10,11},{12,13},{... | collective-permute-start | bytes 196616 | tf_op jit(solution)/shard_map/ppermute | solution.py:206
  29.8 0.6 fusion.4
  30.5 4.3 %collective-permute-done = bf16[128,128]{1,0:T(8,128)(2,1)S(1)} collective-permute-done((bf16[128,128]{1,0:T(8,128)(2,1)S(1)}, bf16[128,128]{1,0:T(8,128)(2,1)S(1)}, u32[]{:S(2)}, u32[]{:S(2)}) %collective-permute-start) | collective-permute-done | bytes 32800 | tf_op jit(solution)/shard_map/ppermute | solution.py:206
  34.8 0.3 convolution_multiply_fusion.1.right_ref
  35.0 0.3 convolution_multiply_fusion.left_ref
  35.3 8.3 %all-to-all-done.entries_ref = bf16[128,16,128]{2,1,0:T(8,128)(2,1)S(1)} async-done(((bf16[128,16,128]{2,1,0:T(8,128)(2,1)}), bf16[128,16,128]{2,1,0:T(8,128)(2,1)S(1)}, u32[]{:S(2)}, u32[]{:S(2)}) %all-to-all-start) | async-done | bytes 524320 | tf_op jit(solution)/shard_map/all_to_all | solution.py:210
  43.7 0.8 shard_map.47
  44.5 0.0 copy-start.2
  44.5 28.4 %all_to_all.20.polar_ref = bf16[128,16,128]{2,1,0:T(8,128)(2,1)S(1)} all-to-all(bf16[128,16,128]{2,1,0:T(8,128)(2,1)S(1)} %get-tuple-element.21), channel_id=1, replica_groups=mesh['energy'=128,'slab'=4] {'energy'}, dimensions={0} | all-to-all | bytes 1048576 | tf_op jit(solution)/shard_map/all_to_all | solution.py:210
  72.9 1.3 shard_map.48
  74.2 28.1 %all_to_all.21.entries_ref = bf16[128,16,128]{2,1,0:T(8,128)(2,1)S(1)} all-to-all(bf16[128,16,128]{2,1,0:T(8,128)(2,1)S(1)} %shard_map.48), channel_id=1, replica_groups=mesh['energy'=128,'slab'=4] {'energy'}, dimensions={0} | all-to-all | bytes 1048576 | tf_op jit(solution)/shard_map/all_to_all | solution.py:210
  102.3 0.7 shard_map.49
  103.0 27.7 %all_to_all.22.sigma_ref = bf16[128,16,128]{2,1,0:T(8,128)(2,1)S(1)} all-to-all(bf16[128,16,128]{2,1,0:T(8,128)(2,1)S(1)} %shard_map.49), channel_id=1, replica_groups=mesh['energy'=128,'slab'=4] {'energy'}, dimensions={0} | all-to-all | bytes 1048576 | tf_op jit(solution)/shard_map/all_to_all | solution.py:210
  130.7 1.6 %shard_map.50 = bf16[512,512]{1,0:T(8,128)(2,1)} custom-call(bf16[128,16,128]{2,1,0:T(8,128)(2,1)S(1)} %all_to_all.22.sigma_ref, bf16[512,512]{1,0:T(8,128)(2,1)S(1)} %bitcast.12, f32[128,128]{1,0:T(8,128)S(1)} %convolution_multiply_fusion.1.right_ref, f32[128,128]{1,0:T(8,128)S(1)} %convolution_multiply_fusion.left_ref), custom_call_target="tpu_custom_call" | custom-call | tf_op jit(solution)/shard_map/pallas_call | solution.py:266
  (15 shorter events, 0.1 us)
Async XLA Ops:
  0.0 1.0 copy-start
  2.0 21.0 %copy-start.1 = (bf16[1,1,512,512]{3,2,1,0:T(8,128)(2,1)S(1)}, bf16[1,1,512,512]{3,2,1,0:T(8,128)(2,1)}, u32[]{:S(2)}) copy-start(bf16[1,1,512,512]{3,2,1,0:T(8,128)(2,1)} %param.4) | copy-start | bytes 1572868
  2.0 41.7 %all-to-all-start = ((bf16[128,16,128]{2,1,0:T(8,128)(2,1)}), bf16[128,16,128]{2,1,0:T(8,128)(2,1)S(1)}, u32[]{:S(2)}, u32[]{:S(2)}) async-start(bf16[128,16,128]{2,1,0:T(8,128)(2,1)} %shard_map.46), calls=%async_computation | async-start | bytes 1048576 | tf_op jit(solution)/shard_map/all_to_all | solution.py:210
  23.0 2.9 %copy-start.4 = (bf16[1,128,8]{1,2,0:T(8,128)(2,1)S(1)}, bf16[1,128,8]{1,2,0:T(8,128)(2,1)}, u32[]{:S(2)}) copy-start(bf16[1,128,8]{1,2,0:T(8,128)(2,1)} %param.7) | copy-start | bytes 6148
  23.0 11.8 %collective-permute-start = (bf16[128,128]{1,0:T(8,128)(2,1)S(1)}, bf16[128,128]{1,0:T(8,128)(2,1)S(1)}, u32[]{:S(2)}, u32[]{:S(2)}) collective-permute-start(bf16[128,128]{1,0:T(8,128)(2,1)S(1)} %get-tuple-element.26), channel_id=1, source_target_pairs={{1,0},{2,1},{3,2},{5,4},{6,5},{7,6},{9,8},{10,9},{11,10},{13,12},{... | collective-permute-start | bytes 98312 | tf_op jit(solution)/shard_map/ppermute | solution.py:206
  25.9 0.7 copy-start.3
  27.1 8.0 %collective-permute-start.1 = (bf16[256,128]{1,0:T(8,128)(2,1)S(1)}, bf16[256,128]{1,0:T(8,128)(2,1)S(1)}, u32[]{:S(2)}, u32[]{:S(2)}) collective-permute-start(bf16[256,128]{1,0:T(8,128)(2,1)S(1)} %pad_maximum_fusion.1), channel_id=1, source_target_pairs={{0,1},{1,2},{2,3},{4,5},{5,6},{6,7},{8,9},{9,10},{10,11},{12,13},{... | collective-permute-start | bytes 196616 | tf_op jit(solution)/shard_map/ppermute | solution.py:206
  44.5 28.5 %copy-start.2 = (bf16[1,512,512]{2,1,0:T(8,128)(2,1)S(1)}, bf16[1,512,512]{2,1,0:T(8,128)(2,1)}, u32[]{:S(2)}) copy-start(bf16[1,512,512]{2,1,0:T(8,128)(2,1)} %param.5) | copy-start | bytes 1572868
